TPU v7x, 128 devices: a whole 4x4x4 slice. The times are simulated.
128 devices in a mesh: section: 4 (over x_hi, core), dp: 32 (over y, x_lo, z).
Axes of the slice: x: 4 (x_hi: 2, x_lo: 2; x = x_hi * 2 + x_lo), y: 4, z: 4, core: 2. Of those that a mesh axis runs over, the one named last changes fastest.
Arguments:
- inputs: bfloat16 [2, 2048, 8192], P(None, 'dp')
- cotangent: bfloat16 [2, 2048, 8192], P(None, 'dp'), may hold values from -6 to 6
- down_weight: bfloat16 [4, 8192, 128], P('section', 'dp'), may hold values from -0.0625 to 0.0625
- up_weight: bfloat16 [4, 8192, 128], P('section', 'dp'), may hold values from -0.5 to 0.5
- section_gains: bfloat16 [4, 8192], P('section'), may hold values from 0.5 to 1.5
- act_bases: bfloat16 [4, 2, 2, 2048, 8192], P('section', None, None, 'dp'), as said below
- grad_bases: bfloat16 [4, 2, 2, 2048, 8192], P('section', None, None, 'dp'), as said below
- slot_ids: int32 [32, 2], P('dp'), may hold values from 0 to 1, each once within a row
- act_exps: int32 [4, 2, 2048, 64], P('section', None, 'dp'), may hold values from 6 to 9
- grad_exps: int32 [4, 2, 2048, 64], P('section', None, 'dp'), may hold values from 6 to 9
Outputs:
- grad_down: float32 [4, 8192, 128], P('section', 'dp')
- grad_up: float32 [4, 8192, 128], P('section', 'dp')
Inputs may be any that keep to these rules, and one draw needn't show every extreme that they name: Each row names every cache slot once: replica r's micro-batch m uses slot slot_ids[r, m]. act_bases[s, 1] equals act_bases[s + 1, 0] for every section s below 3. grad_bases[s, 0] equals grad_bases[s - 1, 1] for every section s from 1 on.
All inputs are finite; a program needn't handle non-finite values.
Results may differ from a plain program's by a relative error of at most 0.034.
Values may be sent and summed in bfloat16 or wider, within the bound.
A program may use at most 128 MiB of HBM per device.

v0:
```python
import math

import jax
import jax.numpy as jnp
from jax import lax
from jax.sharding import PartitionSpec as P

code_limit = 448.0
norm_eps = 1e-05


def from_behind(block, axis, distance):
    devices = range(lax.axis_size(axis))
    route = [(i - distance, i) for i in devices if i - distance in devices]
    return lax.ppermute(block, axis, route)


def power_table(exponents, direction_sign):
    factors = jnp.zeros(exponents.shape, jnp.float32)
    for exponent in range(6, 10):
        factors = jnp.where(
            exponents == exponent, jnp.float32(2.0 ** (direction_sign * exponent)), factors
        )
    return factors


def encode(delta, exponents):
    full_shape = delta.shape
    grouped = delta.reshape(
        full_shape[:-1] + (exponents.shape[-1], full_shape[-1] // exponents.shape[-1])
    )
    scaled = grouped * power_table(exponents, 1)[..., None]
    return jnp.clip(scaled, -code_limit, code_limit).astype(jnp.bfloat16).reshape(full_shape)


def decode(base, codes, exponents):
    full_shape = codes.shape
    grouped = codes.astype(jnp.float32).reshape(
        full_shape[:-1] + (exponents.shape[-1], full_shape[-1] // exponents.shape[-1])
    )
    restored = (grouped * power_table(exponents, -1)[..., None]).reshape(full_shape)
    return (base.astype(jnp.float32) + restored).astype(jnp.bfloat16)


def section_forward(section_input, down_full, up_full, gain):
    full_input = section_input.astype(jnp.float32)
    inverse = lax.rsqrt(jnp.mean(full_input * full_input, axis=-1, keepdims=True) + norm_eps)
    normed = (full_input * inverse * gain.astype(jnp.float32)).astype(jnp.bfloat16)
    inner = jnp.dot(normed, down_full, preferred_element_type=jnp.float32)
    hidden = jax.nn.silu(inner).astype(jnp.bfloat16)
    output = full_input + jnp.dot(hidden, up_full.T, preferred_element_type=jnp.float32)
    return (output, (full_input, inverse, normed, inner, hidden))


def section_backward(upstream, pieces, down_full, up_full, gain):
    full_input, inverse, normed, inner, hidden = pieces
    back_hidden = jnp.dot(upstream, up_full, preferred_element_type=jnp.float32)
    sigma = jax.nn.sigmoid(inner)
    back_inner = (back_hidden * sigma * (1.0 + inner * (1.0 - sigma))).astype(jnp.bfloat16)
    back_normed = jnp.dot(
        back_inner, down_full.T, preferred_element_type=jnp.float32
    ) * gain.astype(jnp.float32)
    back_input = (
        upstream.astype(jnp.float32)
        + inverse * back_normed
        - full_input * inverse**3 * jnp.mean(back_normed * full_input, axis=-1, keepdims=True)
    )
    return (back_input, back_inner)


def store_row(table, value, batch_index, is_valid):
    kept = jnp.where(is_valid, value, table[batch_index])
    return lax.dynamic_update_index_in_dim(table, kept, batch_index, 0)


def body(
    inputs,
    cotangent,
    down_weight,
    up_weight,
    section_gains,
    act_bases,
    grad_bases,
    slot_ids,
    act_exps,
    grad_exps,
):
    sections = lax.axis_size("section")
    replicas = lax.axis_size("dp")
    section_index = lax.axis_index("section")
    down_full, up_full = (
        lax.all_gather(down_weight[0], "dp", axis=0, tiled=True),
        lax.all_gather(up_weight[0], "dp", axis=0, tiled=True),
    )
    gain = section_gains[0]
    micro_count, tok_rows, model_width = inputs.shape
    rank = down_full.shape[1]
    block_count = act_exps.shape[-1]
    step_count = micro_count + sections - 1
    is_first = section_index == 0
    is_last = section_index == sections - 1
    stored = jnp.zeros((micro_count, tok_rows, model_width), jnp.bfloat16)
    codes_in = jnp.zeros((tok_rows, model_width), jnp.bfloat16)
    exps_in = jnp.zeros((tok_rows, block_count), jnp.int32)
    for step_number in range(step_count):
        batch_raw = step_number - section_index
        is_valid = (batch_raw >= 0) & (batch_raw < micro_count)
        batch_index = jnp.clip(batch_raw, 0, micro_count - 1)
        slot_index = slot_ids[0, batch_index]
        received = decode(act_bases[0, 0, slot_index], codes_in, exps_in)
        section_input = jnp.where(is_first, inputs[batch_index], received)
        stored = store_row(stored, section_input, batch_index, is_valid)
        output, pieces = section_forward(section_input, down_full, up_full, gain)
        if step_number + 1 < step_count:
            codes = encode(
                output - act_bases[0, 1, slot_index].astype(jnp.float32), act_exps[0, batch_index]
            )
            codes_in, exps_in = from_behind((codes, act_exps[0, batch_index]), "section", 1)
    down_total = jnp.zeros((model_width, rank), jnp.float32)
    up_total = jnp.zeros((model_width, rank), jnp.float32)
    codes_in = jnp.zeros((tok_rows, model_width), jnp.bfloat16)
    exps_in = jnp.zeros((tok_rows, block_count), jnp.int32)
    for step_number in range(step_count):
        batch_raw = step_number - (sections - 1 - section_index)
        is_valid = (batch_raw >= 0) & (batch_raw < micro_count)
        batch_index = jnp.clip(batch_raw, 0, micro_count - 1)
        slot_index = slot_ids[0, batch_index]
        received = decode(grad_bases[0, 1, slot_index], codes_in, exps_in)
        upstream = jnp.where(is_last, cotangent[batch_index], received)
        upstream = jnp.where(is_valid, upstream, jnp.zeros_like(upstream))
        pieces = section_forward(stored[batch_index], down_full, up_full, gain)[1]
        back_input, back_inner = section_backward(upstream, pieces, down_full, up_full, gain)
        down_total = down_total + jnp.dot(
            pieces[2].T, back_inner, preferred_element_type=jnp.float32
        )
        up_total = up_total + jnp.dot(upstream.T, pieces[4], preferred_element_type=jnp.float32)
        if step_number + 1 < step_count:
            codes = encode(
                back_input - grad_bases[0, 0, slot_index].astype(jnp.float32),
                grad_exps[0, batch_index],
            )
            codes_in, exps_in = from_behind((codes, grad_exps[0, batch_index]), "section", -1)
    grad_scale = 1.0 / math.sqrt(micro_count * tok_rows * replicas)
    down_share, up_share = (
        lax.psum_scatter(
            down_total.astype(jnp.bfloat16), "dp", scatter_dimension=0, tiled=True
        ).astype(jnp.float32),
        lax.psum_scatter(
            up_total.astype(jnp.bfloat16), "dp", scatter_dimension=0, tiled=True
        ).astype(jnp.float32),
    )
    return ((down_share * grad_scale)[None], (up_share * grad_scale)[None])


def solution(mesh):
    return jax.shard_map(
        body,
        mesh=mesh,
        in_specs=(
            P(None, "dp", None),
            P(None, "dp", None),
            P("section", "dp", None),
            P("section", "dp", None),
            P("section", None),
            P("section", None, None, "dp", None),
            P("section", None, None, "dp", None),
            P("dp", None),
            P("section", None, "dp", None),
            P("section", None, "dp", None),
        ),
        out_specs=(P("section", "dp", None), P("section", "dp", None)),
        check_vma=False,
    )
```

profile of v0, /device:TPU:2, one launch (start us, length us, event | category | flops | bytes accessed | tf_op | source)
XLA Modules:
  0.0 880.2 jit_solution(6902892176044585667)
XLA Ops:
  12.5 4.4 collective-permute-start.3
  32.4 127.7 %all-gather.5.cloned.1.call-done = bf16[1,8192,128]{2,1,0:T(8,128)(2,1)} async-done(((bf16[1,256,128]{2,1,0:T(8,128)(2,1)}), bf16[1,8192,128]{2,1,0:T(8,128)(2,1)}) %all-gather.5.cloned.1.call-update) | async-done | bytes 2097168 | tf_op jit(solution)/shard_map/all_gather | solution.py:92
  160.1 154.9 %all-gather.7.cloned.1.call-done = bf16[1,8192,128]{2,1,0:T(8,128)(2,1)} async-done(((bf16[1,256,128]{2,1,0:T(8,128)(2,1)}), bf16[1,8192,128]{2,1,0:T(8,128)(2,1)}) %all-gather.7.cloned.1.call-update) | async-done | bytes 2097168 | tf_op jit(solution)/shard_map/all_gather | solution.py:93
  316.9 7.6 fusion.14
  340.9 4.6 fusion.24
  347.4 6.9 fusion.15
  354.3 4.0 collective-permute-start.2
  362.1 4.2 fusion.27
  368.3 6.9 fusion.16
  375.2 13.2 %collective-permute-start.4 = (bf16[64,8192]{1,0:T(8,128)(2,1)}, bf16[64,8192]{1,0:T(8,128)(2,1)S(1)}, u32[]{:S(2)}, u32[]{:S(2)}) collective-permute-start(bf16[64,8192]{1,0:T(8,128)(2,1)} %fusion.16), channel_id=1, source_target_pairs={{0,32},{32,64},{64,96},{1,33},{33,65},{65,97},{2,34},{34,66},{66,9... | collective-permute-start | bytes 3145736 | tf_op jit(solution)/shard_map/ppermute | solution.py:15
  391.8 4.2 fusion.30
  398.0 6.9 fusion.17
  404.9 15.1 %collective-permute-start.6 = (bf16[64,8192]{1,0:T(8,128)(2,1)}, bf16[64,8192]{1,0:T(8,128)(2,1)S(1)}, u32[]{:S(2)}, u32[]{:S(2)}) collective-permute-start(bf16[64,8192]{1,0:T(8,128)(2,1)} %fusion.17), channel_id=1, source_target_pairs={{0,32},{32,64},{64,96},{1,33},{33,65},{65,97},{2,34},{34,66},{66,9... | collective-permute-start | bytes 3145736 | tf_op jit(solution)/shard_map/ppermute | solution.py:15
  423.1 3.1 fusion.178
  431.3 4.3 fusion.41
  449.7 3.7 collective-permute-done.9
  458.8 3.3 fusion.180
  469.8 14.9 %collective-permute-done.10 = bf16[64,8192]{1,0:T(8,128)(2,1)S(1)} collective-permute-done((bf16[64,8192]{1,0:T(8,128)(2,1)S(1)}, bf16[64,8192]{1,0:T(8,128)(2,1)S(1)}, u32[]{:S(2)}, u32[]{:S(2)}) %collective-permute-start.10) | collective-permute-done | bytes 1048608 | tf_op jit(solution)/shard_map/ppermute | solution.py:15
  494.6 14.3 %collective-permute-done.12 = bf16[64,8192]{1,0:T(8,128)(2,1)S(1)} collective-permute-done((bf16[64,8192]{1,0:T(8,128)(2,1)S(1)}, bf16[64,8192]{1,0:T(8,128)(2,1)S(1)}, u32[]{:S(2)}, u32[]{:S(2)}) %collective-permute-start.12) | collective-permute-done | bytes 1048608 | tf_op jit(solution)/shard_map/ppermute | solution.py:15
  519.4 13.8 %collective-permute-done.14 = bf16[64,8192]{1,0:T(8,128)(2,1)S(1)} collective-permute-done((bf16[64,8192]{1,0:T(8,128)(2,1)S(1)}, bf16[64,8192]{1,0:T(8,128)(2,1)S(1)}, u32[]{:S(2)}, u32[]{:S(2)}) %collective-permute-start.14) | collective-permute-done | bytes 1048608 | tf_op jit(solution)/shard_map/ppermute | solution.py:15
  540.9 2.8 convolution_add_fusion.5
  543.8 5.5 fusion
  549.2 161.3 %reduce-scatter.5.cloned.1.call-done = bf16[256,128]{1,0:T(8,128)(2,1)} async-done(((bf16[8192,128]{1,0:T(8,128)(2,1)}), bf16[256,128]{1,0:T(8,128)(2,1)}) %reduce-scatter.5.cloned.1.call-update) | async-done | bytes 65552 | tf_op jit(solution)/shard_map/reduce_scatter | solution.py:148
  712.0 159.9 %reduce-scatter.3.cloned.1.call-done = bf16[256,128]{1,0:T(8,128)(2,1)} async-done(((bf16[8192,128]{1,0:T(8,128)(2,1)}), bf16[256,128]{1,0:T(8,128)(2,1)}) %reduce-scatter.3.cloned.1.call-update) | async-done | bytes 65552 | tf_op jit(solution)/shard_map/reduce_scatter | solution.py:145
  (154 shorter events, 98.9 us)
Async XLA Ops:
  7.2 152.9 %all-gather.5.cloned.1.call-start = ((), (), s32[]{:S(2)}) async-start(), calls=%async_computation.4 | async-start | bytes 2162688 | tf_op jit(solution)/shard_map/all_gather | solution.py:92
  7.9 307.0 %all-gather.7.cloned.1.call-start = ((), (), s32[]{:S(2)}) async-start(), calls=%async_computation.5 | async-start | bytes 2162688 | tf_op jit(solution)/shard_map/all_gather | solution.py:93
  8.6 701.9 %reduce-scatter.5.cloned.1.call-start = ((), (), s32[]{:S(2)}) async-start(), calls=%async_computation.3 | async-start | bytes 2162688 | tf_op jit(solution)/shard_map/reduce_scatter | solution.py:148
  10.2 326.7 %collective-permute-start.1 = (s32[64,64]{1,0:T(8,128)}, s32[64,64]{1,0:T(8,128)}, u32[]{:S(2)}, u32[]{:S(2)}) collective-permute-start(s32[64,64]{1,0:T(8,128)} %get-tuple-element.38), channel_id=1, source_target_pairs={{0,32},{32,64},{64,96},{1,33},{33,65},{65,97},{2,34},{34,66},{66,9... | collective-permute-start | bytes 49160 | tf_op jit(solution)/shard_map/ppermute | solution.py:15
  12.5 325.4 %collective-permute-start.3 = (s32[64,64]{1,0:T(8,128)S(1)}, s32[64,64]{1,0:T(8,128)}, u32[]{:S(2)}, u32[]{:S(2)}) collective-permute-start(s32[64,64]{1,0:T(8,128)S(1)} %get-tuple-element.36), channel_id=1, source_target_pairs={{0,32},{32,64},{64,96},{1,33},{33,65},{65,97},{2,34},{34,66},{66,9... | collective-permute-start | bytes 49160 | tf_op jit(solution)/shard_map/ppermute | solution.py:15
  16.9 321.8 %collective-permute-start.5 = (s32[64,64]{1,0:T(8,128)S(1)}, s32[64,64]{1,0:T(8,128)}, u32[]{:S(2)}, u32[]{:S(2)}) collective-permute-start(s32[64,64]{1,0:T(8,128)S(1)} %get-tuple-element.40), channel_id=1, source_target_pairs={{0,32},{32,64},{64,96},{1,33},{33,65},{65,97},{2,34},{34,66},{66,9... | collective-permute-start | bytes 49160 | tf_op jit(solution)/shard_map/ppermute | solution.py:15
  18.8 320.6 %collective-permute-start.7 = (s32[64,64]{1,0:T(8,128)S(1)}, s32[64,64]{1,0:T(8,128)}, u32[]{:S(2)}, u32[]{:S(2)}) collective-permute-start(s32[64,64]{1,0:T(8,128)S(1)} %get-tuple-element.18), channel_id=1, source_target_pairs={{0,32},{32,64},{64,96},{1,33},{33,65},{65,97},{2,34},{34,66},{66,9... | collective-permute-start | bytes 49160 | tf_op jit(solution)/shard_map/ppermute | solution.py:15
  324.5 15.8 %collective-permute-start = (bf16[64,8192]{1,0:T(8,128)(2,1)}, bf16[64,8192]{1,0:T(8,128)(2,1)}, u32[]{:S(2)}, u32[]{:S(2)}) collective-permute-start(bf16[64,8192]{1,0:T(8,128)(2,1)} %fusion.14), channel_id=1, source_target_pairs={{0,32},{32,64},{64,96},{1,33},{33,65},{65,97},{2,34},{34,66},{66,9... | collective-permute-start | bytes 3145736 | tf_op jit(solution)/shard_map/ppermute | solution.py:15
  354.3 6.9 collective-permute-start.2
  375.2 15.8 %collective-permute-start.4 = (bf16[64,8192]{1,0:T(8,128)(2,1)}, bf16[64,8192]{1,0:T(8,128)(2,1)S(1)}, u32[]{:S(2)}, u32[]{:S(2)}) collective-permute-start(bf16[64,8192]{1,0:T(8,128)(2,1)} %fusion.16), channel_id=1, source_target_pairs={{0,32},{32,64},{64,96},{1,33},{33,65},{65,97},{2,34},{34,66},{66,9... | collective-permute-start | bytes 3145736 | tf_op jit(solution)/shard_map/ppermute | solution.py:15
  404.9 17.3 %collective-permute-start.6 = (bf16[64,8192]{1,0:T(8,128)(2,1)}, bf16[64,8192]{1,0:T(8,128)(2,1)S(1)}, u32[]{:S(2)}, u32[]{:S(2)}) collective-permute-start(bf16[64,8192]{1,0:T(8,128)(2,1)} %fusion.17), channel_id=1, source_target_pairs={{0,32},{32,64},{64,96},{1,33},{33,65},{65,97},{2,34},{34,66},{66,9... | collective-permute-start | bytes 3145736 | tf_op jit(solution)/shard_map/ppermute | solution.py:15
  431.3 5.6 copy-start.14
  431.3 6.9 copy-start.13
  431.3 8.2 copy-start.12
  435.6 22.6 %collective-permute-start.8 = (bf16[64,8192]{1,0:T(8,128)(2,1)}, bf16[64,8192]{1,0:T(8,128)(2,1)}, u32[]{:S(2)}, u32[]{:S(2)}) collective-permute-start(bf16[64,8192]{1,0:T(8,128)(2,1)} %fusion.41), channel_id=1, source_target_pairs={{32,0},{64,32},{96,64},{33,1},{65,33},{97,65},{34,2},{66,34},{98,6... | collective-permute-start | bytes 3145736 | tf_op jit(solution)/shard_map/ppermute | solution.py:15
  436.9 16.5 %collective-permute-start.9 = (s32[64,64]{1,0:T(8,128)S(1)}, s32[64,64]{1,0:T(8,128)}, u32[]{:S(2)}, u32[]{:S(2)}) collective-permute-start(s32[64,64]{1,0:T(8,128)S(1)} %copy-done.14), channel_id=1, source_target_pairs={{32,0},{64,32},{96,64},{33,1},{65,33},{97,65},{34,2},{66,34},{98,6... | collective-permute-start | bytes 49160 | tf_op jit(solution)/shard_map/ppermute | solution.py:15
  438.2 17.0 %collective-permute-start.11 = (s32[64,64]{1,0:T(8,128)S(1)}, s32[64,64]{1,0:T(8,128)S(1)}, u32[]{:S(2)}, u32[]{:S(2)}) collective-permute-start(s32[64,64]{1,0:T(8,128)S(1)} %copy-done.13), channel_id=1, source_target_pairs={{32,0},{64,32},{96,64},{33,1},{65,33},{97,65},{34,2},{66,34},{98,6... | collective-permute-start | bytes 49160 | tf_op jit(solution)/shard_map/ppermute | solution.py:15
  439.5 29.6 %collective-permute-start.13 = (s32[64,64]{1,0:T(8,128)S(1)}, s32[64,64]{1,0:T(8,128)S(1)}, u32[]{:S(2)}, u32[]{:S(2)}) collective-permute-start(s32[64,64]{1,0:T(8,128)S(1)} %copy-done.12), channel_id=1, source_target_pairs={{32,0},{64,32},{96,64},{33,1},{65,33},{97,65},{34,2},{66,34},{98,6... | collective-permute-start | bytes 49160 | tf_op jit(solution)/shard_map/ppermute | solution.py:15
  440.8 28.4 %collective-permute-start.15 = (s32[64,64]{1,0:T(8,128)S(1)}, s32[64,64]{1,0:T(8,128)S(1)}, u32[]{:S(2)}, u32[]{:S(2)}) collective-permute-start(s32[64,64]{1,0:T(8,128)S(1)} %get-tuple-element.8), channel_id=1, source_target_pairs={{32,0},{64,32},{96,64},{33,1},{65,33},{97,65},{34,2},{66,34},{98,6... | collective-permute-start | bytes 49160 | tf_op jit(solution)/shard_map/ppermute | solution.py:15
  467.4 17.3 %collective-permute-start.10 = (bf16[64,8192]{1,0:T(8,128)(2,1)S(1)}, bf16[64,8192]{1,0:T(8,128)(2,1)S(1)}, u32[]{:S(2)}, u32[]{:S(2)}) collective-permute-start(bf16[64,8192]{1,0:T(8,128)(2,1)S(1)} %fusion.51), channel_id=1, source_target_pairs={{32,0},{64,32},{96,64},{33,1},{65,33},{97,65},{34,2},{66,34},{98,6... | collective-permute-start | bytes 3145736 | tf_op jit(solution)/shard_map/ppermute | solution.py:15
  469.3 16.0 %copy-start.10 = (bf16[2,64,8192]{2,1,0:T(8,128)(2,1)S(1)}, bf16[2,64,8192]{2,1,0:T(8,128)(2,1)}, u32[]{:S(2)}) copy-start(bf16[2,64,8192]{2,1,0:T(8,128)(2,1)} %param.11) | copy-start | bytes 6291460
  491.3 17.6 %collective-permute-start.12 = (bf16[64,8192]{1,0:T(8,128)(2,1)S(1)}, bf16[64,8192]{1,0:T(8,128)(2,1)S(1)}, u32[]{:S(2)}, u32[]{:S(2)}) collective-permute-start(bf16[64,8192]{1,0:T(8,128)(2,1)S(1)} %fusion.61), channel_id=1, source_target_pairs={{32,0},{64,32},{96,64},{33,1},{65,33},{97,65},{34,2},{66,34},{98,6... | collective-permute-start | bytes 3145736 | tf_op jit(solution)/shard_map/ppermute | solution.py:15
  515.5 17.6 %collective-permute-start.14 = (bf16[64,8192]{1,0:T(8,128)(2,1)S(1)}, bf16[64,8192]{1,0:T(8,128)(2,1)S(1)}, u32[]{:S(2)}, u32[]{:S(2)}) collective-permute-start(bf16[64,8192]{1,0:T(8,128)(2,1)S(1)} %fusion.71), channel_id=1, source_target_pairs={{32,0},{64,32},{96,64},{33,1},{65,33},{97,65},{34,2},{66,34},{98,6... | collective-permute-start | bytes 3145736 | tf_op jit(solution)/shard_map/ppermute | solution.py:15
  537.7 334.2 %reduce-scatter.3.cloned.1.call-start = ((), (), s32[]{:S(2)}) async-start(), calls=%async_computation.2 | async-start | bytes 2162688 | tf_op jit(solution)/shard_map/reduce_scatter | solution.py:145
  (16 other events, 45.5 us)
Sparse Core Ops, SparseCore 0:
  9.6 150.3 all-gather.4
  161.7 153.1 all-gather.6
  537.8 172.6 reduce-scatter.4
  712.9 158.9 reduce-scatter.2
where the time goes:
time: 897 us; the launch traced here: 880 us
  waiting for transfers between devices  653 us (73%)
  other arithmetic  56.8 us (6%)
  starting transfers between devices  56.7 us (6%)
  matrix products  55.7 us (6%)
  between operations  33.9 us (4%)
  local copies, waits for them, and re-layouts  23.6 us (3%)
    reduce_scatter x1, waiting for transfers between devices, body(): lax.psum_scatter(up_total.astype(jnp.bfloat16), 'dp', scatter_dimension=0...  161 us
    reduce_scatter x1, waiting for transfers between devices, body(): lax.psum_scatter(down_total.astype(jnp.bfloat16), 'dp', scatter_dimension...  160 us
    all_gather x1, waiting for transfers between devices, body(): lax.all_gather(up_weight[0], 'dp', axis=0, tiled=True)  155 us
    all_gather x1, waiting for transfers between devices, body(): lax.all_gather(down_weight[0], 'dp', axis=0, tiled=True)  128 us
    ppermute x16, starting transfers between devices, from_behind(): return lax.ppermute(block, axis, route)  56.6 us
    ppermute x16, waiting for transfers between devices, from_behind(): return lax.ppermute(block, axis, route)  48.3 us
    dot_general x4, matrix products, section_forward(): jnp.dot(hidden, up_full.T, preferred_element_type=jnp.float32)  28.2 us
  transfers between devices with their start and end apart: 20, of which 10 were waited for; matrix products, arithmetic and copies ran while one was open for 7% of the time, Pallas kernels for 0%

commit v1 on v0

v1 whole, which is shorter than its diff:
```python
import functools
import math

import jax
import jax.numpy as jnp
from jax import lax
from jax.experimental import pallas as pl
from jax.experimental.pallas import tpu as pltpu
from jax.sharding import PartitionSpec as P

MESH = pl.DeviceIdType.MESH
F32 = jnp.float32
BF16 = jnp.bfloat16

SECTIONS = 4
WIDTH = 8192
RANK = 128
TOK = 64
ROWS = 2 * TOK
CH = 256
CHUNKS = 8
NORM_EPS = 1e-05
OFF = (1, 3, 2)
DOWN, UP = 0, 1


def dot(a, b):
    return jnp.dot(a, b, preferred_element_type=F32)


def dot_t(a, b):
    return lax.dot_general(a, b, (((1,), (1,)), ((), ())), preferred_element_type=F32)


def kernel(
    x_hbm,
    ct_hbm,
    dw_hbm,
    uw_hbm,
    ab_hbm,
    gb_hbm,
    gain_ref,
    lim_ref,
    slot_ref,
    od_ref,
    ou_ref,
    W,
    acts,
    ups,
    TB,
    GB,
    gains,
    lims,
    sel,
    xs,
    xr,
    inner_all,
    inv_all,
    hid_all,
    bis_all,
    G,
    R1d,
    R1u,
    S1d,
    S1u,
    R2,
    S2,
    R3,
    loc_sem,
    base_s,
    base_r,
    small_s,
    small_r,
    p0_s,
    p0_r,
    p1_s,
    p1_r,
    p2_s,
    p2_r,
    r1_s,
    r1_r,
    r2_s,
    r2_r,
    r3_s,
    r3_r,
    x_s,
    x_r,
):
    S, J = lax.axis_index("section"), lax.axis_index("dp")
    xh, c = S // 2, S % 2
    y, xl, z = J // 8, (J // 4) % 2, J % 4
    i_own = z // 2
    src = (z % 2) == c
    not_src = (z % 2) != c

    def dp(yy, xx, zz):
        return yy * 8 + xx * 4 + zz

    def at_y(o):
        return (S, dp((y + o) % 4, xl, z))

    def at_z(o):
        return (S, dp(y, xl, (z + o) % 4))

    def group(e):
        return ((S + e) % 4, J)

    p0_sec = xl * 2 + z % 2

    def p0_dev(xx):
        return (p0_sec, dp(y, xx, z))

    def p0_self(xx):
        return (p0_sec == S) & (xl == xx)

    def owner(s):
        return (s, dp(y, xh, z))

    def owner_self(s):
        return (S == s) & (xl == xh)

    def feat(kk, h, cc):
        return (kk // 2) * 2048 + h * 1024 + ((kk % 2) * 2 + cc) * 256

    def remote(a, b, ss, rs, dev):
        return pltpu.make_async_remote_copy(
            src_ref=a, dst_ref=b, send_sem=ss, recv_sem=rs, device_id=dev, device_id_type=MESH
        )

    def arrived(ref, rs):
        remote(ref, ref, rs, rs, (S, J)).wait_recv()

    def sent(ref, ss):
        remote(ref, ref, ss, ss, (S, J)).wait_send()

    def local_done(ref, sem):
        pltpu.make_async_copy(ref, ref, sem).wait()

    barrier = pltpu.get_barrier_semaphore()

    def greet(dev):
        pl.semaphore_signal(barrier, inc=1, device_id=dev, device_id_type=MESH)

    for e in (1, 2, 3):
        greet(group(e))
        greet(at_y(e))
        greet(at_z(e))
    for xx in (0, 1):
        @pl.when(jnp.logical_not(p0_self(xx)))
        def _():
            greet(p0_dev(xx))
    for s in range(SECTIONS):
        @pl.when(src & jnp.logical_not(owner_self(s)))
        def _():
            greet(owner(s))

    def load(ref_of, dst, sem, h, cc):
        def step(kk, _):
            pltpu.make_async_copy(
                ref_of.at[:, pl.ds(pl.multiple_of(feat(kk, h, cc), 256), CH)], dst.at[kk], sem
            ).start()
            return 0

        lax.fori_loop(0, CHUNKS, step, 0)

    def push(ref_of, dst, ss, rs, h, cc, dev):
        def step(kk, _):
            remote(
                ref_of.at[:, pl.ds(pl.multiple_of(feat(kk, h, cc), 256), CH)],
                dst.at[kk],
                ss,
                rs,
                dev,
            ).start()
            return 0

        lax.fori_loop(0, CHUNKS, step, 0)

    near = 2 * xh
    far = 2 - near
    holds_mid = c != xh
    lacks_mid = c == xh
    load(x_hbm, acts.at[0], loc_sem.at[0], xh, c)

    is_self0 = jnp.where(p0_self(0) | p0_self(1), 1, 0)
    own_any = jnp.where(xl == xh, 1, 0)
    n_greet = 9 + 2 - is_self0 + jnp.where(src, 4 - own_any, 0)
    pl.semaphore_wait(barrier, n_greet)

    for xx in (0, 1):
        for mat, ref in ((DOWN, dw_hbm), (UP, uw_hbm)):
            there = W.at[S, mat, y, i_own]

            @pl.when(jnp.logical_not(p0_self(xx)))
            def _():
                remote(ref, there, p0_s.at[xx, mat], p0_r.at[S, mat], p0_dev(xx)).start()

            @pl.when(p0_self(xx))
            def _():
                pltpu.make_async_copy(ref, there, p0_r.at[S, mat]).start()

    for e in (1, 2, 3):
        remote(gain_ref, gains.at[S], small_s.at[e - 1, 0], small_r.at[e - 1, 0], group(e)).start()
        remote(lim_ref, lims.at[S], small_s.at[e - 1, 1], small_r.at[e - 1, 1], group(e)).start()

    cross = (S + 2) % 4
    sib = xh * 2 + (1 - c)
    push(ab_hbm.at[1 - c], TB.at[near], base_s.at[0], base_r.at[0], 1 - xh, c, (cross, J))
    load(ab_hbm.at[1 - c], TB.at[near], loc_sem.at[2], xh, c)

    @pl.when(holds_mid)
    def _():
        push(ab_hbm.at[c], TB.at[1], base_s.at[1], base_r.at[1], xh, 1 - c, (sib, J))
        load(ab_hbm.at[c], TB.at[1], loc_sem.at[3], xh, c)

    load(ct_hbm, ups.at[3], loc_sem.at[1], xh, c)
    push(gb_hbm.at[1 - c], GB.at[near], base_s.at[2], base_r.at[2], 1 - xh, c, (cross, J))
    load(gb_hbm.at[1 - c], GB.at[near], loc_sem.at[4], xh, c)

    @pl.when(holds_mid)
    def _():
        push(gb_hbm.at[c], GB.at[1], base_s.at[3], base_r.at[3], xh, 1 - c, (sib, J))
        load(gb_hbm.at[c], GB.at[1], loc_sem.at[5], xh, c)

    gains[S] = gain_ref[...]
    lims[S] = lim_ref[...]

    def build_sel(kk, _):
        b0 = (kk // 2) * 16 + xh * 8 + (kk % 2) * 4 + c * 2
        row = lax.broadcasted_iota(jnp.int32, (128, CH), 0)
        blk = lax.broadcasted_iota(jnp.int32, (128, CH), 1) // 128 + b0
        sel[0, kk] = jnp.where(row == blk, 1.0, 0.0).astype(BF16)
        sel[1, kk] = jnp.where(row == blk + 64, 1.0, 0.0).astype(BF16)
        return 0

    lax.fori_loop(0, CHUNKS, build_sel, 0)

    def p1_send(s):
        @pl.when(src)
        def _():
            for mat in (DOWN, UP):
                arrived(W.at[s, mat, y, i_own], p0_r.at[s, mat])
            for d, o in enumerate(OFF):
                w = W.at[s, DOWN, y, i_own]
                remote(w, w, p1_s.at[s, DOWN, d], p1_r.at[s, DOWN, d], at_y(o)).start()
                w = W.at[s, UP, y, i_own]
                remote(w, w, p1_s.at[s, UP, d], p1_r.at[s, UP, d], at_z(o)).start()

    def from_z(o):
        return ((z + 4 - o) % 4) // 2

    def z_arrive(view, sems):
        @pl.when(src)
        def _():
            arrived(view(from_z(OFF[2])), sems.at[2])

        @pl.when(not_src)
        def _():
            arrived(view(from_z(OFF[0])), sems.at[0])
            arrived(view(from_z(OFF[1])), sems.at[1])

    def p2_send(s):
        @pl.when(src)
        def _():
            for d, o in enumerate(OFF):
                arrived(W.at[s, DOWN, (y + 4 - o) % 4, i_own], p1_r.at[s, DOWN, d])
            for d, o in enumerate(OFF):
                w = W.at[s, DOWN, :, i_own]
                remote(w, w, p2_s.at[s, DOWN, d], p2_r.at[s, DOWN, d], at_z(o)).start()

        z_arrive(lambda i: W.at[s, UP, y, i], p1_r.at[s, UP])
        for d, o in enumerate(OFF):
            w = W.at[s, UP, y]
            remote(w, w, p2_s.at[s, UP, d], p2_r.at[s, UP, d], at_y(o)).start()

    def down_ready(s):
        z_arrive(lambda i: W.at[s, DOWN, :, i], p2_r.at[s, DOWN])

    def up_ready(s):
        for d, o in enumerate(OFF):
            arrived(W.at[s, UP, (y + 4 - o) % 4], p2_r.at[s, UP, d])

    def rows(m):
        return pl.ds(m * TOK, TOK)

    def gain_row(s, kk):
        return gains[s, pl.ds((kk // 2) * 8 + xh * 4 + (kk % 2) * 2 + c, 1), :]

    def fold(v):
        return v[:, :128] + v[:, 128:]

    def chunk_loop(step, init):
        return lax.fori_loop(0, CHUNKS, step, init, unroll=True)

    def x_send(ex, m):
        for e in (1, 2, 3):
            remote(
                xs.at[ex, m], xr.at[ex, m, e - 1], x_s.at[ex, m, e - 1], x_r.at[ex, m, e - 1], group(e)
            ).start()

    def x_total(ex, m, part):
        total = xs[ex, m, part].astype(F32)
        for e in range(3):
            total = total + xr[ex, m, e, part].astype(F32)
        return total

    def x_wait(ex, m):
        for e in range(3):
            arrived(xr.at[ex, m, e], x_r.at[ex, m, e])

    zero = jnp.zeros((TOK, 128), F32)

    def enter(s, kk, value, inner, sq):
        full = value.astype(F32)
        sq = sq + fold(full * full)
        scaled = (full * gain_row(s, kk)).astype(BF16)
        return inner + dot(scaled, W[s, DOWN, kk // 2, kk % 2]), sq

    def hand_over(ex, m, a, b):
        xs[ex, m, 0] = a.astype(BF16)
        xs[ex, m, 1] = b.astype(BF16)
        x_send(ex, m)

    def first(m):
        def step(kk, carry):
            return enter(0, kk, acts[0, kk, rows(m), :], *carry)

        inner, sq = chunk_loop(step, (zero, zero))
        hand_over(0, m, inner, sq)

    def activate(s, m):
        x_wait(s, m)
        mean = jnp.sum(x_total(s, m, 1), axis=-1, keepdims=True) * (1.0 / WIDTH)
        inv = jnp.broadcast_to(lax.rsqrt(mean + NORM_EPS), (TOK, 128))
        inner = x_total(s, m, 0) * inv
        hid = (inner * jax.nn.sigmoid(inner)).astype(BF16)
        inner_all[s, rows(m), :] = inner
        inv_all[s, rows(m), :] = inv
        hid_all[s, rows(m), :] = hid
        return hid

    def recode(value, table, b, m, kk, limit):
        use_first = jnp.broadcast_to(slot_ref[0:1, :], (TOK, CH)) == m
        base = jnp.where(
            use_first, table[b, kk, 0:TOK, :].astype(F32), table[b, kk, TOK:ROWS, :].astype(F32)
        )
        delta = jnp.minimum(jnp.maximum(value - base, -limit), limit).astype(BF16)
        return (base + delta.astype(F32)).astype(BF16)

    def forward(s, m):
        hid = activate(s, m)
        table = lims[s, rows(m), :]

        def step(kk, carry):
            out = acts[s, kk, rows(m), :].astype(F32) + dot_t(hid, W[s, UP, kk // 2, kk % 2])
            value = recode(out, TB, s, m, kk, dot(table, sel[0, kk]))
            acts[s + 1, kk, rows(m), :] = value
            return enter(s + 1, kk, value, *carry)

        inner, sq = chunk_loop(step, (zero, zero))
        hand_over(s + 1, m, inner, sq)

    def back_first(m):
        def step(kk, carry):
            return carry + dot(ups[3, kk, rows(m), :], W[3, UP, kk // 2, kk % 2])

        xs[4 + 3, m, 0] = chunk_loop(step, zero).astype(BF16)
        xb_send(3, m)

    def xb_send(s, m):
        for e in (1, 2, 3):
            remote(
                xs.at[4 + s, m, 0],
                xr.at[4 + s, m, e - 1, 0],
                x_s.at[4 + s, m, e - 1],
                x_r.at[4 + s, m, e - 1],
                group(e),
            ).start()

    def back_inner(s, m):
        for e in range(3):
            arrived(xr.at[4 + s, m, e, 0], x_r.at[4 + s, m, e])
        inner, inv = inner_all[s, rows(m), :], inv_all[s, rows(m), :]
        sig = jax.nn.sigmoid(inner)
        bi = x_total(4 + s, m, 0) * sig * (1.0 + inner * (1.0 - sig)) * inv
        bis = bi.astype(BF16)
        bis_all[s, rows(m), :] = bis
        coef = jnp.sum(bis.astype(F32) * inner * inv, axis=-1, keepdims=True) * (1.0 / WIDTH)
        return bis, jnp.broadcast_to(coef, (TOK, CH))

    def backward(s, m):
        bis, coef = back_inner(s, m)
        table = lims[s, rows(m), :]

        def step(kk, carry):
            back = dot_t(bis, W[s, DOWN, kk // 2, kk % 2]) * gain_row(s, kk)
            value = (
                ups[s, kk, rows(m), :].astype(F32)
                + back
                - acts[s, kk, rows(m), :].astype(F32) * coef
            )
            value = recode(value, GB, s - 1, m, kk, dot(table, sel[1, kk]))
            ups[s - 1, kk, rows(m), :] = value
            return carry + dot(value, W[s - 1, UP, kk // 2, kk % 2])

        xs[4 + s - 1, m, 0] = chunk_loop(step, zero).astype(BF16)
        xb_send(s - 1, m)

    def grad_up(s):
        left = jnp.transpose(hid_all[s].astype(F32)).astype(BF16)

        def step(kk, _):
            G[s, UP, kk // 2, kk % 2] = dot(left, ups[s, kk]).astype(BF16)
            return 0

        chunk_loop(step, 0)
        for d, o in enumerate(OFF):
            remote(
                G.at[s, UP, (y + o) % 4], R1u.at[s, d], r1_s.at[s, UP, d], r1_r.at[s, UP, d], at_y(o)
            ).start()

    def to_z(o):
        return ((z + o) % 4) // 2

    def z_give(view, there, ss, rs):
        def give(d):
            o = OFF[d]
            remote(view(to_z(o)), there.at[d], ss.at[d], rs.at[d], at_z(o)).start()

        @pl.when(src)
        def _():
            give(2)

        @pl.when(not_src)
        def _():
            give(0)
            give(1)

    def z_given(view, ss):
        @pl.when(src)
        def _():
            sent(view, ss.at[2])

        @pl.when(not_src)
        def _():
            sent(view, ss.at[0])
            sent(view, ss.at[1])

    def grad_down(s):
        left = jnp.transpose(bis_all[s].astype(F32)).astype(BF16)

        def step(kk, _):
            G[s, DOWN, kk // 2, kk % 2] = (dot(left, acts[s, kk]) * gain_row(s, kk)).astype(BF16)
            return 0

        chunk_loop(step, 0)
        z_give(lambda i: G.at[s, DOWN, :, i], R1d.at[s], r1_s.at[s, DOWN], r1_r.at[s, DOWN])

    def add4(a, b):
        return (
            a.astype(F32) + b[0].astype(F32) + (b[1].astype(F32) + b[2].astype(F32))
        ).astype(BF16)

    def r2_up(s):
        for d in range(3):
            arrived(R1u.at[s, d], r1_r.at[s, UP, d])
        for i in range(2):
            S1u[s, i] = add4(G[s, UP, y, i], [R1u[s, d, i] for d in range(3)])
        z_give(lambda i: S1u.at[s, i], R2.at[s, UP], r2_s.at[s, UP], r2_r.at[s, UP])

    def r2_down(s):
        @pl.when(src)
        def _():
            for d in range(3):
                arrived(R1d.at[s, d], r1_r.at[s, DOWN, d])
            for yy in range(4):
                S1d[s, yy] = add4(G[s, DOWN, yy, i_own], [R1d[s, d, yy] for d in range(3)])
            for d, o in enumerate(OFF):
                remote(
                    S1d.at[s, (y + o) % 4],
                    R2.at[s, DOWN, d],
                    r2_s.at[s, DOWN, d],
                    r2_r.at[s, DOWN, d],
                    at_y(o),
                ).start()

    def r3(s, mat):
        @pl.when(src)
        def _():
            for d in range(3):
                arrived(R2.at[s, mat, d], r2_r.at[s, mat, d])
            own = S1u[s, i_own] if mat == UP else S1d[s, y]
            S2[s, mat] = add4(own, [R2[s, mat, d] for d in range(3)])

            @pl.when(jnp.logical_not(owner_self(s)))
            def _():
                remote(
                    S2.at[s, mat], R3.at[xl, mat], r3_s.at[s, mat], r3_r.at[xl, mat], owner(s)
                ).start()

            @pl.when(owner_self(s))
            def _():
                pltpu.make_async_copy(S2.at[s, mat], R3.at[xl, mat], r3_r.at[xl, mat]).start()

    for s in range(SECTIONS):
        p1_send(s)
    for s in range(SECTIONS):
        p2_send(s)
    for e in (1, 2, 3):
        arrived(gains.at[(S + 4 - e) % 4], small_r.at[e - 1, 0])
        arrived(lims.at[(S + 4 - e) % 4], small_r.at[e - 1, 1])
    local_done(acts.at[0], loc_sem.at[0])
    down_ready(0)
    first(0)
    first(1)

    def base_ready(table, b, near_sem, mid_sem, far_sem, mid_far_sem):
        if b == 1:
            @pl.when(holds_mid)
            def _():
                local_done(table.at[1], mid_sem)

            @pl.when(lacks_mid)
            def _():
                arrived(table.at[1], mid_far_sem)
        else:
            @pl.when(near == b)
            def _():
                local_done(table.at[b], near_sem)

            @pl.when(near != b)
            def _():
                arrived(table.at[b], far_sem)

    for s in range(SECTIONS - 1):
        up_ready(s)
        base_ready(TB, s, loc_sem.at[2], loc_sem.at[3], base_r.at[0], base_r.at[1])
        down_ready(s + 1)
        forward(s, 0)
        forward(s, 1)
    up_ready(3)
    local_done(ups.at[3], loc_sem.at[1])
    back_first(0)
    back_first(1)
    activate(3, 0)
    activate(3, 1)
    grad_up(3)
    for s in (3, 2, 1):
        base_ready(GB, s - 1, loc_sem.at[4], loc_sem.at[5], base_r.at[2], base_r.at[3])
        backward(s, 0)
        backward(s, 1)
        grad_down(s)
        grad_up(s - 1)
        if s < 3:
            r2_up(s + 1)
            r2_down(s + 1)
        if s < 2:
            r3(s + 2, UP)
            r3(s + 2, DOWN)
    back_inner(0, 0)
    back_inner(0, 1)
    grad_down(0)
    r2_up(0)
    r2_up(1)
    r2_down(1)
    r3(2, UP)
    r3(2, DOWN)
    r2_down(0)
    r3(1, UP)
    r3(1, DOWN)
    r3(0, UP)
    r3(0, DOWN)

    scale = 1.0 / math.sqrt(2 * 2048)
    for mat, out in ((UP, ou_ref), (DOWN, od_ref)):
        for xx in (0, 1):
            arrived(R3.at[xx, mat], r3_r.at[xx, mat])
        total = (R3[0, mat].astype(F32) + R3[1, mat].astype(F32)) * scale
        out[...] = jnp.transpose(total)

    for xx in (0, 1):
        @pl.when(jnp.logical_not(p0_self(xx)))
        def _():
            for mat, ref in ((DOWN, dw_hbm), (UP, uw_hbm)):
                sent(ref, p0_s.at[xx, mat])
    for e in range(3):
        sent(gain_ref, small_s.at[e, 0])
        sent(lim_ref, small_s.at[e, 1])
    sent(TB.at[0], base_s.at[0])
    sent(GB.at[0], base_s.at[2])

    @pl.when(holds_mid)
    def _():
        sent(TB.at[1], base_s.at[1])
        sent(GB.at[1], base_s.at[3])

    def drain(s, _):
        @pl.when(src)
        def _():
            for d in range(3):
                sent(W.at[s, DOWN, y, i_own], p1_s.at[s, DOWN, d])
                sent(W.at[s, UP, y, i_own], p1_s.at[s, UP, d])
                sent(W.at[s, DOWN, :, i_own], p2_s.at[s, DOWN, d])
                sent(S1d.at[s, 0], r2_s.at[s, DOWN, d])

            @pl.when(jnp.logical_not(owner_self(s)))
            def _():
                for mat in (DOWN, UP):
                    sent(S2.at[s, mat], r3_s.at[s, mat])

        for d in range(3):
            sent(W.at[s, UP, y], p2_s.at[s, UP, d])
            sent(G.at[s, UP, 0], r1_s.at[s, UP, d])
        z_given(G.at[s, DOWN, :, 0], r1_s.at[s, DOWN])
        z_given(S1u.at[s, 0], r2_s.at[s, UP])
        for m in (0, 1):
            for e in range(3):
                sent(xs.at[s, m], x_s.at[s, m, e])
                sent(xs.at[4 + s, m, 0], x_s.at[4 + s, m, e])
        return 0

    lax.fori_loop(0, SECTIONS, drain, 0)


def body(
    inputs,
    cotangent,
    down_weight,
    up_weight,
    section_gains,
    act_bases,
    grad_bases,
    slot_ids,
    act_exps,
    grad_exps,
):
    def limits(exps):
        out = jnp.full(exps.shape, 448.0 * 2.0**-6, F32)
        for e in (7, 8, 9):
            out = jnp.where(exps == e, 448.0 * 2.0**-e, out)
        return out.reshape(ROWS, 64).astype(BF16)

    lim = jnp.concatenate([limits(act_exps), limits(grad_exps)], axis=1)
    gain = section_gains.astype(F32).reshape(32, CH)
    slot = jnp.broadcast_to(slot_ids[0, 0], (8, CH))
    any_spec = pl.BlockSpec(memory_space=pl.ANY)
    vmem = pl.BlockSpec(memory_space=pltpu.VMEM)
    dma = pltpu.SemaphoreType.DMA
    grad_down, grad_up = pl.pallas_call(
        kernel,
        out_shape=(jax.ShapeDtypeStruct((CH, RANK), F32),) * 2,
        in_specs=[any_spec] * 6 + [vmem] * 3,
        out_specs=(vmem, vmem),
        scratch_shapes=[
            pltpu.VMEM((4, 2, 4, 2, CH, RANK), BF16),
            pltpu.VMEM((4, CHUNKS, ROWS, CH), BF16),
            pltpu.VMEM((4, CHUNKS, ROWS, CH), BF16),
            pltpu.VMEM((3, CHUNKS, ROWS, CH), BF16),
            pltpu.VMEM((3, CHUNKS, ROWS, CH), BF16),
            pltpu.VMEM((4, 32, CH), F32),
            pltpu.VMEM((4, ROWS, 128), BF16),
            pltpu.VMEM((2, CHUNKS, 128, CH), BF16),
            pltpu.VMEM((8, 2, 2, TOK, 128), BF16),
            pltpu.VMEM((8, 2, 3, 2, TOK, 128), BF16),
            pltpu.VMEM((4, ROWS, RANK), F32),
            pltpu.VMEM((4, ROWS, RANK), F32),
            pltpu.VMEM((4, ROWS, RANK), BF16),
            pltpu.VMEM((4, ROWS, RANK), BF16),
            pltpu.VMEM((4, 2, 4, 2, RANK, CH), BF16),
            pltpu.VMEM((4, 3, 4, RANK, CH), BF16),
            pltpu.VMEM((4, 3, 2, RANK, CH), BF16),
            pltpu.VMEM((4, 4, RANK, CH), BF16),
            pltpu.VMEM((4, 2, RANK, CH), BF16),
            pltpu.VMEM((4, 2, 3, RANK, CH), BF16),
            pltpu.VMEM((4, 2, RANK, CH), BF16),
            pltpu.VMEM((2, 2, RANK, CH), BF16),
            dma((6,)),
            dma((4,)),
            dma((4,)),
            dma((3, 2)),
            dma((3, 2)),
            dma((2, 2)),
            dma((4, 2)),
            dma((4, 2, 3)),
            dma((4, 2, 3)),
            dma((4, 2, 3)),
            dma((4, 2, 3)),
            dma((4, 2, 3)),
            dma((4, 2, 3)),
            dma((4, 2, 3)),
            dma((4, 2, 3)),
            dma((4, 2)),
            dma((2, 2)),
            dma((8, 2, 3)),
            dma((8, 2, 3)),
        ],
        compiler_params=pltpu.CompilerParams(
            collective_id=0, has_side_effects=True, vmem_limit_bytes=56 * 2**20
        ),
    )(
        inputs.reshape(ROWS, WIDTH),
        cotangent.reshape(ROWS, WIDTH),
        down_weight[0],
        up_weight[0],
        act_bases.reshape(2, ROWS, WIDTH),
        grad_bases.reshape(2, ROWS, WIDTH),
        gain,
        lim,
        slot,
    )
    return grad_down[None], grad_up[None]


def solution(mesh):
    return jax.shard_map(
        body,
        mesh=mesh,
        in_specs=(
            P(None, "dp", None),
            P(None, "dp", None),
            P("section", "dp", None),
            P("section", "dp", None),
            P("section", None),
            P("section", None, None, "dp", None),
            P("section", None, None, "dp", None),
            P("dp", None),
            P("section", None, "dp", None),
            P("section", None, "dp", None),
        ),
        out_specs=(P("section", "dp", None), P("section", "dp", None)),
        check_vma=False,
    )
```

time: 897 us -> 113 us (0.13); the launches traced: 880 us -> 113 us
  waiting for transfers between devices: 653 us -> 0 us
  Pallas kernels: 0 us -> 104 us
  starting transfers between devices: 56.7 us -> 0 us
  matrix products: 55.7 us -> 0 us
  other arithmetic: 56.8 us -> 3.26 us
  between operations: 33.9 us -> 0.65 us
  local copies, waits for them, and re-layouts: 23.6 us -> 5 us
    reduce_scatter x2 -> x0, waiting for transfers between devices: 321 us -> none  [the longest x1 161 us: body(): lax.psum_scatter(up_total.astype(jnp.bfloat16), 'dp', scatter_dimension=0...]
    all_gather x2 -> x0, waiting for transfers between devices: 283 us -> none  [the longest x1 155 us: body(): lax.all_gather(up_weight[0], 'dp', axis=0, tiled=True)]
    pallas_call x0 -> x1, Pallas kernels: none -> 104 us  [body(): pl.pallas_call(kernel, out_shape=(jax.ShapeDtypeStruct((CH, RANK), F32),)...]
    ppermute x16 -> x0, starting transfers between devices: 56.6 us -> none  [from_behind(): return lax.ppermute(block, axis, route)]
    dot_general x27 -> x0, matrix products: 55.7 us -> none  [the longest x4 28.2 us: section_forward(): jnp.dot(hidden, up_full.T, preferred_element_type=jnp.float32)]
    ppermute x16 -> x0, waiting for transfers between devices: 48.3 us -> none  [from_behind(): return lax.ppermute(block, axis, route)]
    select_n x15 -> x0, other arithmetic: 16.6 us -> none  [the longest x5 10.4 us: body(): upstream = jnp.where(is_valid, upstream, jnp.zeros_like(upstream))]
    reduce_sum x5 -> x0, other arithmetic: 15.5 us -> none  [section_forward(): jnp.mean(full_input * full_input, axis=-1, keepdims=True) + norm_eps]
  transfers between devices with their start and end apart: 20 -> 0, of which waited for: 10 -> 0; matrix products, arithmetic and copies ran while one was open for 7% -> 0% of each run, Pallas kernels for 0% -> 0%
where the time goes in v1:
time: 113 us
  Pallas kernels  104 us (92%)
  local copies, waits for them, and re-layouts  5 us (4%)
  other arithmetic  3.26 us (3%)
    pallas_call x1, Pallas kernels, body(): pl.pallas_call(kernel, out_shape=(jax.ShapeDtypeStruct((CH, RANK), F32),)...  104 us
    unnamed x2, local copies, waits for them, and re-layouts  3.14 us

profile of v1, /device:TPU:2, one launch (start us, length us, event | category | flops | bytes accessed | tf_op | source)
XLA Modules:
  0.0 112.7 jit_solution(5385966399337457492)
XLA Ops:
  0.6 1.2 %broadcast_in_dim.25.slot_ref = s32[8,256]{1,0:T(8,128)} broadcast(s32[]{:T(128)} %bitcast.22), dimensions={} | broadcast | bytes 8196 | tf_op jit(solution)/shard_map/broadcast_in_dim | solution.py:645
  1.9 0.8 convert_reduce_fusion
  2.7 0.6 reshape.32.gain_ref
  3.3 0.9 select_convert_fusion.1
  4.2 0.9 select_convert_fusion
  5.1 0.7 pad_maximum_fusion.lim_ref
  5.8 103.8 %shard_map.113 = (f32[256,128]{1,0:T(8,128)}, f32[256,128]{1,0:T(8,128)}) custom-call(bf16[128,8192]{1,0:T(8,128)(2,1)} %bitcast.14, bf16[128,8192]{1,0:T(8,128)(2,1)} %bitcast.15, bf16[256,128]{1,0:T(8,128)(2,1)} %bitcast.20, bf16[256,128]{1,0:T(8,128)(2,1)} %bitcast.21, bf16[2,128,8192]{2,1,0:T(8,128)(2,1)} %bitcast.12, bf16[2,128,8192]{2,1,0:T(8,128)(2,1)} %bitcast.13, ...), custom_call_target="tpu_custom_call" | custom-call | tf_op jit(solution)/shard_map/pallas_call | solution.py:649
  109.6 1.6 %copy.14 = f32[1,256,128]{2,1,0:T(8,128)} copy(f32[1,256,128]{2,1,0:T(8,128)} %bitcast.19) | data formatting | bytes 262144
  111.1 1.6 %copy.15 = f32[1,256,128]{2,1,0:T(8,128)} copy(f32[1,256,128]{2,1,0:T(8,128)} %bitcast.18) | data formatting | bytes 262144

commit v2 on v1

--- a/solution.py
+++ b/solution.py
@@ -39,16 +39,18 @@
     uw_hbm,
     ab_hbm,
     gb_hbm,
-    gain_ref,
-    lim_ref,
+    gain_hbm,
+    ae_hbm,
+    ge_hbm,
     slot_ref,
-    od_ref,
-    ou_ref,
+    out_ref,
     W,
     acts,
     ups,
     TB,
     GB,
+    gain_in,
+    exps_in,
     gains,
     lims,
     sel,
@@ -163,7 +165,7 @@
 
         lax.fori_loop(0, CHUNKS, step, 0)
 
-    def push(ref_of, dst, ss, rs, h, cc, dev):
+    def push(ref_of, dst, ss, rs, h, cc, dev, lo, hi):
         def step(kk, _):
             remote(
                 ref_of.at[:, pl.ds(pl.multiple_of(feat(kk, h, cc), 256), CH)],
@@ -174,12 +176,17 @@
             ).start()
             return 0
 
-        lax.fori_loop(0, CHUNKS, step, 0)
+        lax.fori_loop(lo, hi, step, 0)
 
     near = 2 * xh
-    far = 2 - near
     holds_mid = c != xh
     lacks_mid = c == xh
+    cross = (S + 2) % 4
+    sib = xh * 2 + (1 - c)
+
+    pltpu.make_async_copy(gain_hbm, gain_in, loc_sem.at[6]).start()
+    pltpu.make_async_copy(ae_hbm, exps_in.at[0], loc_sem.at[7]).start()
+    pltpu.make_async_copy(ge_hbm, exps_in.at[1], loc_sem.at[8]).start()
     load(x_hbm, acts.at[0], loc_sem.at[0], xh, c)
 
     is_self0 = jnp.where(p0_self(0) | p0_self(1), 1, 0)
@@ -187,8 +194,8 @@
     n_greet = 9 + 2 - is_self0 + jnp.where(src, 4 - own_any, 0)
     pl.semaphore_wait(barrier, n_greet)
 
-    for xx in (0, 1):
-        for mat, ref in ((DOWN, dw_hbm), (UP, uw_hbm)):
+    for mat, ref in ((DOWN, dw_hbm), (UP, uw_hbm)):
+        for xx in (0, 1):
             there = W.at[S, mat, y, i_own]
 
             @pl.when(jnp.logical_not(p0_self(xx)))
@@ -199,31 +206,18 @@
             def _():
                 pltpu.make_async_copy(ref, there, p0_r.at[S, mat]).start()
 
+    pltpu.make_async_copy(gain_hbm, gain_in, loc_sem.at[6]).wait()
+    gains[S] = gain_in[...].astype(F32)
+    pltpu.make_async_copy(ae_hbm, exps_in.at[0], loc_sem.at[7]).wait()
+    pltpu.make_async_copy(ge_hbm, exps_in.at[1], loc_sem.at[8]).wait()
+    exps = jnp.concatenate([exps_in[0], exps_in[1]], axis=1)
+    limit = jnp.full((ROWS, 128), 448.0 * 2.0**-6, F32)
+    for e in (7, 8, 9):
+        limit = jnp.where(exps == e, 448.0 * 2.0**-e, limit)
+    lims[S] = limit.astype(BF16)
     for e in (1, 2, 3):
-        remote(gain_ref, gains.at[S], small_s.at[e - 1, 0], small_r.at[e - 1, 0], group(e)).start()
-        remote(lim_ref, lims.at[S], small_s.at[e - 1, 1], small_r.at[e - 1, 1], group(e)).start()
-
-    cross = (S + 2) % 4
-    sib = xh * 2 + (1 - c)
-    push(ab_hbm.at[1 - c], TB.at[near], base_s.at[0], base_r.at[0], 1 - xh, c, (cross, J))
-    load(ab_hbm.at[1 - c], TB.at[near], loc_sem.at[2], xh, c)
-
-    @pl.when(holds_mid)
-    def _():
-        push(ab_hbm.at[c], TB.at[1], base_s.at[1], base_r.at[1], xh, 1 - c, (sib, J))
-        load(ab_hbm.at[c], TB.at[1], loc_sem.at[3], xh, c)
-
-    load(ct_hbm, ups.at[3], loc_sem.at[1], xh, c)
-    push(gb_hbm.at[1 - c], GB.at[near], base_s.at[2], base_r.at[2], 1 - xh, c, (cross, J))
-    load(gb_hbm.at[1 - c], GB.at[near], loc_sem.at[4], xh, c)
-
-    @pl.when(holds_mid)
-    def _():
-        push(gb_hbm.at[c], GB.at[1], base_s.at[3], base_r.at[3], xh, 1 - c, (sib, J))
-        load(gb_hbm.at[c], GB.at[1], loc_sem.at[5], xh, c)
-
-    gains[S] = gain_ref[...]
-    lims[S] = lim_ref[...]
+        remote(gains.at[S], gains.at[S], small_s.at[e - 1, 0], small_r.at[e - 1, 0], group(e)).start()
+        remote(lims.at[S], lims.at[S], small_s.at[e - 1, 1], small_r.at[e - 1, 1], group(e)).start()
 
     def build_sel(kk, _):
         b0 = (kk // 2) * 16 + xh * 8 + (kk % 2) * 4 + c * 2
@@ -233,18 +227,42 @@
         sel[1, kk] = jnp.where(row == blk + 64, 1.0, 0.0).astype(BF16)
         return 0
 
-    lax.fori_loop(0, CHUNKS, build_sel, 0)
-
-    def p1_send(s):
+    def t_bases():
+        push(ab_hbm.at[1 - c], TB.at[near], base_s.at[0], base_r.at[0], 1 - xh, c, (cross, J), 0, CHUNKS)
+        load(ab_hbm.at[1 - c], TB.at[near], loc_sem.at[2], xh, c)
+
+        @pl.when(holds_mid)
+        def _():
+            push(ab_hbm.at[c], TB.at[1], base_s.at[1], base_r.at[1], xh, 1 - c, (sib, J), 0, CHUNKS)
+            load(ab_hbm.at[c], TB.at[1], loc_sem.at[3], xh, c)
+
+    def g_bases():
+        load(ct_hbm, ups.at[3], loc_sem.at[1], xh, c)
+        load(gb_hbm.at[1 - c], GB.at[near], loc_sem.at[4], xh, c)
+
+        @pl.when(holds_mid)
+        def _():
+            push(gb_hbm.at[c], GB.at[1], base_s.at[3], base_r.at[3], xh, 1 - c, (sib, J), 0, CHUNKS)
+            load(gb_hbm.at[c], GB.at[1], loc_sem.at[5], xh, c)
+
+    def g_cross(lo, hi):
+        push(gb_hbm.at[1 - c], GB.at[near], base_s.at[2], base_r.at[2], 1 - xh, c, (cross, J), lo, hi)
+
+    def p0_left():
+        for mat, ref in ((DOWN, dw_hbm), (UP, uw_hbm)):
+            for xx in (0, 1):
+                @pl.when(jnp.logical_not(p0_self(xx)))
+                def _():
+                    sent(ref, p0_s.at[xx, mat])
+
+    def p1_send(s, mat):
         @pl.when(src)
         def _():
-            for mat in (DOWN, UP):
-                arrived(W.at[s, mat, y, i_own], p0_r.at[s, mat])
+            w = W.at[s, mat, y, i_own]
+            arrived(w, p0_r.at[s, mat])
             for d, o in enumerate(OFF):
-                w = W.at[s, DOWN, y, i_own]
-                remote(w, w, p1_s.at[s, DOWN, d], p1_r.at[s, DOWN, d], at_y(o)).start()
-                w = W.at[s, UP, y, i_own]
-                remote(w, w, p1_s.at[s, UP, d], p1_r.at[s, UP, d], at_z(o)).start()
+                there = at_y(o) if mat == DOWN else at_z(o)
+                remote(w, w, p1_s.at[s, mat, d], p1_r.at[s, mat, d], there).start()
 
     def from_z(o):
         return ((z + 4 - o) % 4) // 2
@@ -259,7 +277,7 @@
             arrived(view(from_z(OFF[0])), sems.at[0])
             arrived(view(from_z(OFF[1])), sems.at[1])
 
-    def p2_send(s):
+    def p2_down(s):
         @pl.when(src)
         def _():
             for d, o in enumerate(OFF):
@@ -268,6 +286,7 @@
                 w = W.at[s, DOWN, :, i_own]
                 remote(w, w, p2_s.at[s, DOWN, d], p2_r.at[s, DOWN, d], at_z(o)).start()
 
+    def p2_up(s):
         z_arrive(lambda i: W.at[s, UP, y, i], p1_r.at[s, UP])
         for d, o in enumerate(OFF):
             w = W.at[s, UP, y]
@@ -284,7 +303,7 @@
         return pl.ds(m * TOK, TOK)
 
     def gain_row(s, kk):
-        return gains[s, pl.ds((kk // 2) * 8 + xh * 4 + (kk % 2) * 2 + c, 1), :]
+        return gains[s, :, pl.ds(pl.multiple_of(feat(kk, xh, c), 256), CH)]
 
     def fold(v):
         return v[:, :128] + v[:, 128:]
@@ -340,7 +359,7 @@
         return hid
 
     def recode(value, table, b, m, kk, limit):
-        use_first = jnp.broadcast_to(slot_ref[0:1, :], (TOK, CH)) == m
+        use_first = jnp.full((TOK, CH), slot_ref[0, m]) == 0
         base = jnp.where(
             use_first, table[b, kk, 0:TOK, :].astype(F32), table[b, kk, TOK:ROWS, :].astype(F32)
         )
@@ -502,10 +521,39 @@
             def _():
                 pltpu.make_async_copy(S2.at[s, mat], R3.at[xl, mat], r3_r.at[xl, mat]).start()
 
-    for s in range(SECTIONS):
-        p1_send(s)
-    for s in range(SECTIONS):
-        p2_send(s)
+    def base_ready(table, b, near_sem, mid_sem, far_sem, mid_far_sem):
+        if b == 1:
+            @pl.when(holds_mid)
+            def _():
+                local_done(table.at[1], mid_sem)
+
+            @pl.when(lacks_mid)
+            def _():
+                arrived(table.at[1], mid_far_sem)
+        else:
+            @pl.when(near == b)
+            def _():
+                local_done(table.at[b], near_sem)
+
+            @pl.when(near != b)
+            def _():
+                arrived(table.at[b], far_sem)
+
+    lax.fori_loop(0, CHUNKS, build_sel, 0)
+    for mat in (DOWN, UP):
+        for s in (0, 1):
+            p1_send(s, mat)
+    p0_left()
+    t_bases()
+    p2_down(0)
+    for s in (2, 3):
+        for mat in (DOWN, UP):
+            p1_send(s, mat)
+    g_bases()
+    p2_up(0)
+    for s in (1, 2, 3):
+        p2_down(s)
+        p2_up(s)
     for e in (1, 2, 3):
         arrived(gains.at[(S + 4 - e) % 4], small_r.at[e - 1, 0])
         arrived(lims.at[(S + 4 - e) % 4], small_r.at[e - 1, 1])
@@ -513,31 +561,15 @@
     down_ready(0)
     first(0)
     first(1)
-
-    def base_ready(table, b, near_sem, mid_sem, far_sem, mid_far_sem):
-        if b == 1:
-            @pl.when(holds_mid)
-            def _():
-                local_done(table.at[1], mid_sem)
-
-            @pl.when(lacks_mid)
-            def _():
-                arrived(table.at[1], mid_far_sem)
-        else:
-            @pl.when(near == b)
-            def _():
-                local_done(table.at[b], near_sem)
-
-            @pl.when(near != b)
-            def _():
-                arrived(table.at[b], far_sem)
-
+    g_cross(0, 3)
     for s in range(SECTIONS - 1):
         up_ready(s)
         base_ready(TB, s, loc_sem.at[2], loc_sem.at[3], base_r.at[0], base_r.at[1])
         down_ready(s + 1)
         forward(s, 0)
         forward(s, 1)
+        if s < 2:
+            g_cross(3 * s + 3, min(3 * s + 6, CHUNKS))
     up_ready(3)
     local_done(ups.at[3], loc_sem.at[1])
     back_first(0)
@@ -551,41 +583,28 @@
         backward(s, 1)
         grad_down(s)
         grad_up(s - 1)
-        if s < 3:
-            r2_up(s + 1)
-            r2_down(s + 1)
-        if s < 2:
-            r3(s + 2, UP)
-            r3(s + 2, DOWN)
+    r2_up(3)
     back_inner(0, 0)
     back_inner(0, 1)
     grad_down(0)
-    r2_up(0)
-    r2_up(1)
-    r2_down(1)
-    r3(2, UP)
-    r3(2, DOWN)
-    r2_down(0)
-    r3(1, UP)
-    r3(1, DOWN)
-    r3(0, UP)
-    r3(0, DOWN)
+    r2_down(3)
+    for s in (2, 1, 0):
+        r2_up(s)
+        r2_down(s)
+    for s in (3, 2, 1, 0):
+        r3(s, UP)
+        r3(s, DOWN)
 
     scale = 1.0 / math.sqrt(2 * 2048)
-    for mat, out in ((UP, ou_ref), (DOWN, od_ref)):
+    for mat in (UP, DOWN):
         for xx in (0, 1):
             arrived(R3.at[xx, mat], r3_r.at[xx, mat])
         total = (R3[0, mat].astype(F32) + R3[1, mat].astype(F32)) * scale
-        out[...] = jnp.transpose(total)
-
-    for xx in (0, 1):
-        @pl.when(jnp.logical_not(p0_self(xx)))
-        def _():
-            for mat, ref in ((DOWN, dw_hbm), (UP, uw_hbm)):
-                sent(ref, p0_s.at[xx, mat])
+        out_ref[mat] = jnp.transpose(total)
+
     for e in range(3):
-        sent(gain_ref, small_s.at[e, 0])
-        sent(lim_ref, small_s.at[e, 1])
+        sent(gains.at[0], small_s.at[e, 0])
+        sent(lims.at[0], small_s.at[e, 1])
     sent(TB.at[0], base_s.at[0])
     sent(GB.at[0], base_s.at[2])
 
@@ -620,6 +639,11 @@
         return 0
 
     lax.fori_loop(0, SECTIONS, drain, 0)
+
+
+def split(both_ref, down_ref, up_ref):
+    down_ref[0] = both_ref[DOWN]
+    up_ref[0] = both_ref[UP]
 
 
 def body(
@@ -634,30 +658,23 @@
     act_exps,
     grad_exps,
 ):
-    def limits(exps):
-        out = jnp.full(exps.shape, 448.0 * 2.0**-6, F32)
-        for e in (7, 8, 9):
-            out = jnp.where(exps == e, 448.0 * 2.0**-e, out)
-        return out.reshape(ROWS, 64).astype(BF16)
-
-    lim = jnp.concatenate([limits(act_exps), limits(grad_exps)], axis=1)
-    gain = section_gains.astype(F32).reshape(32, CH)
-    slot = jnp.broadcast_to(slot_ids[0, 0], (8, CH))
     any_spec = pl.BlockSpec(memory_space=pl.ANY)
     vmem = pl.BlockSpec(memory_space=pltpu.VMEM)
     dma = pltpu.SemaphoreType.DMA
-    grad_down, grad_up = pl.pallas_call(
+    both = pl.pallas_call(
         kernel,
-        out_shape=(jax.ShapeDtypeStruct((CH, RANK), F32),) * 2,
-        in_specs=[any_spec] * 6 + [vmem] * 3,
-        out_specs=(vmem, vmem),
+        out_shape=jax.ShapeDtypeStruct((2, CH, RANK), F32),
+        in_specs=[any_spec] * 9 + [pl.BlockSpec(memory_space=pltpu.SMEM)],
+        out_specs=vmem,
         scratch_shapes=[
             pltpu.VMEM((4, 2, 4, 2, CH, RANK), BF16),
             pltpu.VMEM((4, CHUNKS, ROWS, CH), BF16),
             pltpu.VMEM((4, CHUNKS, ROWS, CH), BF16),
             pltpu.VMEM((3, CHUNKS, ROWS, CH), BF16),
             pltpu.VMEM((3, CHUNKS, ROWS, CH), BF16),
-            pltpu.VMEM((4, 32, CH), F32),
+            pltpu.VMEM((1, WIDTH), BF16),
+            pltpu.VMEM((2, ROWS, 64), jnp.int32),
+            pltpu.VMEM((4, 1, WIDTH), F32),
             pltpu.VMEM((4, ROWS, 128), BF16),
             pltpu.VMEM((2, CHUNKS, 128, CH), BF16),
             pltpu.VMEM((8, 2, 2, TOK, 128), BF16),
@@ -674,7 +691,7 @@
             pltpu.VMEM((4, 2, 3, RANK, CH), BF16),
             pltpu.VMEM((4, 2, RANK, CH), BF16),
             pltpu.VMEM((2, 2, RANK, CH), BF16),
-            dma((6,)),
+            dma((9,)),
             dma((4,)),
             dma((4,)),
             dma((3, 2)),
@@ -704,11 +721,18 @@
         up_weight[0],
         act_bases.reshape(2, ROWS, WIDTH),
         grad_bases.reshape(2, ROWS, WIDTH),
-        gain,
-        lim,
-        slot,
+        section_gains,
+        act_exps.reshape(ROWS, 64),
+        grad_exps.reshape(ROWS, 64),
+        slot_ids,
     )
-    return grad_down[None], grad_up[None]
+    grad_down, grad_up = pl.pallas_call(
+        split,
+        out_shape=(jax.ShapeDtypeStruct((1, CH, RANK), F32),) * 2,
+        in_specs=[vmem],
+        out_specs=(vmem, vmem),
+    )(both)
+    return grad_down, grad_up
 
 
 def solution(mesh):

time: 113 us -> 99.5 us (0.88)
  Pallas kernels: 104 us -> 98.6 us
  local copies, waits for them, and re-layouts: 5 us -> 0 us
  other arithmetic: 3.26 us -> 0 us
    pallas_call x1 -> x2, Pallas kernels: 104 us -> 98.6 us  [the longest x1 97 us: body(): pl.pallas_call(kernel, out_shape=jax.ShapeDtypeStruct((2, CH, RANK), F32)...]
    unnamed x2 -> x0, local copies, waits for them, and re-layouts: 3.14 us -> none
    convert_element_type x2 -> x0, other arithmetic: 1.72 us -> none  [limits(): return out.reshape(ROWS, 64).astype(BF16)]
    broadcast_in_dim x1 -> x0, local copies, waits for them, and re-layouts: 1.24 us -> none  [body(): slot = jnp.broadcast_to(slot_ids[0, 0], (8, CH))]
where the time goes in v2:
time: 99.5 us; the launch traced here: 99.3 us
  Pallas kernels  98.6 us (99%)
    pallas_call x1, Pallas kernels, body(): pl.pallas_call(kernel, out_shape=jax.ShapeDtypeStruct((2, CH, RANK), F32)...  97 us

profile of v2, /device:TPU:2, one launch (start us, length us, event | category | flops | bytes accessed | tf_op | source)
XLA Modules:
  0.0 99.3 jit_solution(17928613457534872600)
XLA Ops:
  0.6 97.0 %shard_map.113.both_ref = f32[2,256,128]{2,1,0:T(8,128)} custom-call(bf16[128,8192]{1,0:T(8,128)(2,1)} %bitcast.10, bf16[128,8192]{1,0:T(8,128)(2,1)} %bitcast.11, bf16[256,128]{1,0:T(8,128)(2,1)} %bitcast.12, bf16[256,128]{1,0:T(8,128)(2,1)} %bitcast.13, bf16[2,128,8192]{2,1,0:T(8,128)(2,1)} %bitcast.8, bf16[2,128,8192]{2,1,0:T(8,128)(2,1)} %bitcast.9, ...), custom_call_target="tpu_custom_call" | custom-call | tf_op jit(solution)/shard_map/pallas_call | solution.py:664
  97.6 1.7 %shard_map.114 = (f32[1,256,128]{2,1,0:T(8,128)}, f32[1,256,128]{2,1,0:T(8,128)}) custom-call(f32[2,256,128]{2,1,0:T(8,128)} %shard_map.113.both_ref), custom_call_target="tpu_custom_call" | custom-call | tf_op jit(solution)/shard_map/pallas_call | solution.py:729

commit v3 on v2

v3 whole, which is shorter than its diff:
```python
import functools
import math

import jax
import jax.numpy as jnp
from jax import lax
from jax.experimental import pallas as pl
from jax.experimental.pallas import tpu as pltpu
from jax.sharding import PartitionSpec as P

MESH = pl.DeviceIdType.MESH
F32 = jnp.float32
BF16 = jnp.bfloat16

SECTIONS = 4
WIDTH = 8192
RANK = 128
TOK = 64
ROWS = 2 * TOK
CH = 256
CHUNKS = 8
NORM_EPS = 1e-05
OFF = (1, 3, 2)
DOWN, UP = 0, 1
(
    L_P0,
    L_GAIN,
    L_LIM,
    L_BASE,
    L_W1,
    L_W0,
    L_WD,
    L_WU,
    L_RU,
    L_RD,
    L_RA,
    L_RB,
    L_R2U,
    L_R2D,
    L_R2L,
    L_R3,
    L_X,
    LEFT_KINDS,
) = range(18)


def dot(a, b):
    return jnp.dot(a, b, preferred_element_type=F32)


def dot_t(a, b):
    return lax.dot_general(a, b, (((1,), (1,)), ((), ())), preferred_element_type=F32)


def kernel(
    x_hbm,
    ct_hbm,
    dw_hbm,
    uw_hbm,
    ab_hbm,
    gb_hbm,
    gain_hbm,
    ae_hbm,
    ge_hbm,
    slot_ref,
    out_ref,
    W,
    acts,
    ups,
    TB,
    GB,
    gain_in,
    exps_in,
    gains,
    lims,
    sel,
    xs,
    xr,
    inner_all,
    inv_all,
    hid_all,
    bis_all,
    G,
    R1d,
    R1u,
    S1d,
    S1u,
    R2,
    S2,
    R3,
    R1h,
    S1h,
    Qd,
    Qu,
    LX,
    wide,
    narrow,
    loc_sem,
    t_ready,
    g_ready,
    gain_r,
    lim_r,
    p0_r,
    p1_r,
    h1_r,
    h2_r,
    p2_r,
    p2b_r,
    q_r,
    r1_r,
    g1_r,
    r2_r,
    r3_r,
    x_r,
    left,
):
    S, J = lax.axis_index("section"), lax.axis_index("dp")
    xh, c = S // 2, S % 2
    y, xl, z = J // 8, (J // 4) % 2, J % 4
    i_own = z // 2
    src = (z % 2) == c
    not_src = (z % 2) != c

    def dp(yy, xx, zz):
        return yy * 8 + xx * 4 + zz

    def at_y(o):
        return (S, dp((y + o) % 4, xl, z))

    def at_z(o):
        return (S, dp(y, xl, (z + o) % 4))

    def group(e):
        return ((S + e) % 4, J)

    p0_sec = xl * 2 + z % 2

    def p0_dev(xx):
        return (p0_sec, dp(y, xx, z))

    def p0_self(xx):
        return (p0_sec == S) & (xl == xx)

    def owner(s):
        return (s, dp(y, xh, z))

    def owner_self(s):
        return (S == s) & (xl == xh)

    def feat(kk, h, cc):
        return (kk // 2) * 2048 + h * 1024 + ((kk % 2) * 2 + cc) * 256

    def remote(a, b, ss, rs, dev):
        return pltpu.make_async_remote_copy(
            src_ref=a, dst_ref=b, send_sem=ss, recv_sem=rs, device_id=dev, device_id_type=MESH
        )

    def arrived(ref, rs):
        remote(ref, ref, rs, rs, (S, J)).wait_recv()

    def sent(ref, ss):
        remote(ref, ref, ss, ss, (S, J)).wait_send()

    def local_done(ref, sem):
        pltpu.make_async_copy(ref, ref, sem).wait()

    barrier = pltpu.get_barrier_semaphore()

    def greet(dev):
        pl.semaphore_signal(barrier, inc=1, device_id=dev, device_id_type=MESH)

    for e in (1, 2, 3):
        greet(group(e))
        greet(at_y(e))
        greet(at_z(e))
    for xx in (0, 1):
        @pl.when(jnp.logical_not(p0_self(xx)))
        def _():
            greet(p0_dev(xx))
    for s in range(SECTIONS):
        @pl.when(src & jnp.logical_not(owner_self(s)))
        def _():
            greet(owner(s))

    def load(ref_of, dst, sem, h, cc):
        def step(kk, _):
            pltpu.make_async_copy(
                ref_of.at[:, pl.ds(pl.multiple_of(feat(kk, h, cc), 256), CH)], dst.at[kk], sem
            ).start()
            return 0

        lax.fori_loop(0, CHUNKS, step, 0)

    def push(ref_of, dst, ss, rs, h, cc, dev, lo, hi):
        def step(kk, _):
            remote(
                ref_of.at[:, pl.ds(pl.multiple_of(feat(kk, h, cc), 256), CH)],
                dst.at[kk],
                ss,
                rs,
                dev,
            ).start()
            return 0

        lax.fori_loop(lo, hi, step, 0)

    near = 2 * xh
    holds_mid = c != xh
    lacks_mid = c == xh
    cross = (S + 2) % 4
    sib = xh * 2 + (1 - c)

    pltpu.make_async_copy(gain_hbm, gain_in, loc_sem.at[2]).start()
    pltpu.make_async_copy(ae_hbm, exps_in.at[0], loc_sem.at[3]).start()
    pltpu.make_async_copy(ge_hbm, exps_in.at[1], loc_sem.at[3]).start()
    load(x_hbm, acts.at[0], loc_sem.at[0], xh, c)

    is_self0 = jnp.where(p0_self(0) | p0_self(1), 1, 0)
    own_any = jnp.where(xl == xh, 1, 0)
    n_greet = 9 + 2 - is_self0 + jnp.where(src, 4 - own_any, 0)
    pl.semaphore_wait(barrier, n_greet)

    def p0_send():
        for mat, ref in ((DOWN, dw_hbm), (UP, uw_hbm)):
            for xx in (0, 1):
                there = W.at[S, mat, y, i_own]

                @pl.when(jnp.logical_not(p0_self(xx)))
                def _():
                    remote(ref, there, left.at[L_P0], p0_r.at[S, mat], p0_dev(xx)).start()

                @pl.when(p0_self(xx))
                def _():
                    pltpu.make_async_copy(ref, there, p0_r.at[S, mat]).start()

    pl.when(c == 0)(p0_send)

    pltpu.make_async_copy(gain_hbm, gain_in, loc_sem.at[2]).wait()
    gains[S] = gain_in[...].astype(F32)
    local_done(exps_in, loc_sem.at[3])
    exps = jnp.concatenate([exps_in[0], exps_in[1]], axis=1)
    limit = jnp.full((ROWS, 128), 448.0 * 2.0**-6, F32)
    for e in (7, 8, 9):
        limit = jnp.where(exps == e, 448.0 * 2.0**-e, limit)
    lims[S] = limit.astype(BF16)
    pl.when(c == 1)(p0_send)
    for e in (1, 2, 3):
        remote(gains.at[S], gains.at[S], left.at[L_GAIN], gain_r.at[0], group(e)).start()
        remote(lims.at[S], lims.at[S], left.at[L_LIM], lim_r.at[0], group(e)).start()

    def build_sel(kk, _):
        b0 = (kk // 2) * 16 + xh * 8 + (kk % 2) * 4 + c * 2
        row = lax.broadcasted_iota(jnp.int32, (128, CH), 0)
        blk = lax.broadcasted_iota(jnp.int32, (128, CH), 1) // 128 + b0
        sel[0, kk] = jnp.where(row == blk, 1.0, 0.0).astype(BF16)
        sel[1, kk] = jnp.where(row == blk + 64, 1.0, 0.0).astype(BF16)
        return 0

    def t_bases():
        push(ab_hbm.at[1 - c], TB.at[near], left.at[L_BASE], t_ready.at[near], 1 - xh, c, (cross, J), 0, CHUNKS)
        load(ab_hbm.at[1 - c], TB.at[near], t_ready.at[near], xh, c)

        @pl.when(holds_mid)
        def _():
            push(ab_hbm.at[c], TB.at[1], left.at[L_BASE], t_ready.at[1], xh, 1 - c, (sib, J), 0, CHUNKS)
            load(ab_hbm.at[c], TB.at[1], t_ready.at[1], xh, c)

    def g_bases():
        load(ct_hbm, ups.at[3], loc_sem.at[1], xh, c)
        load(gb_hbm.at[1 - c], GB.at[near], g_ready.at[near], xh, c)

        @pl.when(holds_mid)
        def _():
            push(gb_hbm.at[c], GB.at[1], left.at[L_BASE], g_ready.at[1], xh, 1 - c, (sib, J), 0, CHUNKS)
            load(gb_hbm.at[c], GB.at[1], g_ready.at[1], xh, c)

    def g_cross(lo, hi):
        push(gb_hbm.at[1 - c], GB.at[near], left.at[L_BASE], g_ready.at[near], 1 - xh, c, (cross, J), lo, hi)

    def p0_left():
        keeps = p0_self(0) | p0_self(1)

        @pl.when(keeps)
        def _():
            sent(W.at[0, 0, 0], left.at[L_P0])

        @pl.when(jnp.logical_not(keeps))
        def _():
            sent(W.at[0, 0, 0:2], left.at[L_P0])

    half = CH // 2
    low, high = pl.ds(0, half), pl.ds(half, half)
    SIDES = ((0, 1), (1, 3))

    def z_take(one, two, sem):
        pl.when(src)(lambda: arrived(one, sem))
        pl.when(not_src)(lambda: arrived(two, sem))

    def p1_send(s, mat):
        @pl.when(src)
        def _():
            w = W.at[s, mat, y, i_own]
            arrived(w, p0_r.at[s, mat])
            for o in OFF:
                there = at_y(o) if mat == DOWN else at_z(o)
                remote(w, w, left.at[L_W1], p1_r.at[s, mat], there).start()

    def p1_first():
        @pl.when(src)
        def _():
            w = W.at[0, DOWN, y, i_own]
            arrived(w, p0_r.at[0, DOWN])
            for o in OFF:
                v = w.at[low]
                remote(v, v, left.at[L_W1], p1_r.at[0, DOWN], at_y(o)).start()
                v = w.at[high]
                remote(v, v, left.at[L_W1], h1_r.at[0], at_z(o)).start()

    def p2_first():
        @pl.when(src)
        def _():
            arrived(W.at[0, DOWN, 0:3, 0, low], p1_r.at[0, DOWN])
            for o in OFF:
                w = W.at[0, DOWN, :, i_own, low]
                remote(w, w, left.at[L_W0], p2_r.at[0, DOWN], at_z(o)).start()

        z_take(W.at[0, DOWN, 0, 0, high], W.at[0, DOWN, 0, :, high], h1_r.at[0])
        for o in OFF:
            w = W.at[0, DOWN, y, :, high]
            remote(w, w, left.at[L_W0], h2_r.at[0], at_y(o)).start()

    def first_ready():
        z_take(W.at[0, DOWN, :, 0, low], W.at[0, DOWN, :, :, low], p2_r.at[0, DOWN])
        arrived(W.at[0, DOWN, 0:3, :, high], h2_r.at[0])

    def p2_down(s):
        @pl.when(src)
        def _():
            arrived(W.at[s, DOWN, 0:3, 0], p1_r.at[s, DOWN])
            for o in (1, 3):
                w = W.at[s, DOWN, :, i_own]
                remote(w, w, left.at[L_WD], p2_r.at[s, DOWN], at_z(o)).start()

    def p3_down(s):
        @pl.when(not_src)
        def _():
            arrived(W.at[s, DOWN], p2_r.at[s, DOWN])
            for d, o in SIDES:
                w = W.at[s, DOWN, pair(d), ((z + 4 - o) % 4) // 2]
                remote(w, w, left.at[L_WD], p2_r.at[s, DOWN], at_z(o)).start()

    def down_ready(s):
        pl.when(src)(lambda: arrived(W.at[s, DOWN, :, 0], p2_r.at[s, DOWN]))

    def p2_up(s):
        z_take(W.at[s, UP, 0, 0], W.at[s, UP, 0], p1_r.at[s, UP])
        for o in OFF if s == 0 else (1, 3):
            w = W.at[s, UP, y]
            remote(w, w, left.at[L_WU], p2_r.at[s, UP], at_y(o)).start()

    def p3_up(s):
        arrived(W.at[s, UP, 0:2], p2_r.at[s, UP])
        for d, o in SIDES:
            w = W.at[s, UP, (y + 4 - o) % 4, d]
            remote(w, w, left.at[L_WU], p2b_r.at[s], at_y(o)).start()

    def up_ready(s):
        if s == 0:
            arrived(W.at[s, UP, 0:3], p2_r.at[s, UP])
        else:
            arrived(W.at[s, UP, 0], p2b_r.at[s])

    def pair(d):
        return pl.ds(2 * d, 2)

    def rows(m):
        return pl.ds(m * TOK, TOK)

    def gain_row(s, kk):
        return gains[s, :, pl.ds(pl.multiple_of(feat(kk, xh, c), 256), CH)]

    def fold(v):
        return v[:, :128] + v[:, 128:]

    def chunk_loop(step, init):
        return lax.fori_loop(0, CHUNKS, step, init, unroll=True)

    def x_send(ex, m):
        for e in (1, 2, 3):
            remote(
                xs.at[ex, m], xr.at[ex, m, e - 1], left.at[L_X], x_r.at[ex, m], group(e)
            ).start()

    def x_total(ex, m, part):
        total = xs[ex, m, part].astype(F32)
        for e in range(3):
            total = total + xr[ex, m, e, part].astype(F32)
        return total

    def x_wait(ex, m):
        arrived(xr.at[ex, m], x_r.at[ex, m])

    zero = jnp.zeros((TOK, 128), F32)

    def enter(s, kk, value, inner, sq):
        full = value.astype(F32)
        sq = sq + fold(full * full)
        scaled = (full * gain_row(s, kk)).astype(BF16)
        return inner + dot(scaled, W[s, DOWN, kk // 2, kk % 2]), sq

    def hand_over(ex, m, a, b):
        xs[ex, m, 0] = a.astype(BF16)
        xs[ex, m, 1] = b.astype(BF16)
        x_send(ex, m)

    def first(m):
        def step(kk, carry):
            return enter(0, kk, acts[0, kk, rows(m), :], *carry)

        inner, sq = chunk_loop(step, (zero, zero))
        hand_over(0, m, inner, sq)

    def activate(s, m):
        x_wait(s, m)
        mean = jnp.sum(x_total(s, m, 1), axis=-1, keepdims=True) * (1.0 / WIDTH)
        inv = jnp.broadcast_to(lax.rsqrt(mean + NORM_EPS), (TOK, 128))
        inner = x_total(s, m, 0) * inv
        hid = (inner * jax.nn.sigmoid(inner)).astype(BF16)
        inner_all[s, rows(m), :] = inner
        inv_all[s, rows(m), :] = inv
        hid_all[s, rows(m), :] = hid
        return hid

    def spread(t, s):
        def step(kk, _):
            LX[t, s - t, kk] = dot(lims[s], sel[t, kk]).astype(BF16)
            return 0

        chunk_loop(step, 0)

    def order(table, b):
        straight = jnp.full((TOK, CH), slot_ref[0, 0]) == 0

        def step(kk, _):
            one = table[b, kk, 0:TOK, :].astype(F32)
            two = table[b, kk, TOK:ROWS, :].astype(F32)
            table[b, kk, 0:TOK, :] = jnp.where(straight, one, two).astype(BF16)
            table[b, kk, TOK:ROWS, :] = jnp.where(straight, two, one).astype(BF16)
            return 0

        chunk_loop(step, 0)

    def recode(value, base, limit):
        base, limit = base.astype(F32), limit.astype(F32)
        delta = jnp.minimum(jnp.maximum(value - base, -limit), limit).astype(BF16)
        return (base + delta.astype(F32)).astype(BF16)

    def cols(kk):
        return pl.ds(pl.multiple_of(kk * CH, CH), CH)

    def flat(s, mat):
        return W[s, mat].reshape(CHUNKS * CH, RANK)

    def forward(s, m):
        hid = activate(s, m)
        wide[...] = dot_t(hid, flat(s, UP))

        def step(kk, sq):
            out = acts[s, kk, rows(m), :].astype(F32) + wide[:, cols(kk)]
            value = recode(out, TB[s, kk, rows(m), :], LX[0, s, kk, rows(m), :])
            acts[s + 1, kk, rows(m), :] = value
            full = value.astype(F32)
            narrow[:, cols(kk)] = (full * gain_row(s + 1, kk)).astype(BF16)
            return sq + fold(full * full)

        sq = chunk_loop(step, zero)
        hand_over(s + 1, m, dot(narrow[...], flat(s + 1, DOWN)), sq)

    def back_first(m):
        def step(kk, carry):
            return carry + dot(ups[3, kk, rows(m), :], W[3, UP, kk // 2, kk % 2])

        xs[4 + 3, m, 0] = chunk_loop(step, zero).astype(BF16)
        xb_send(3, m)

    def xb_send(s, m):
        for e in (1, 2, 3):
            remote(
                xs.at[4 + s, m, 0],
                xr.at[4 + s, m, e - 1, 0],
                left.at[L_X],
                x_r.at[4 + s, m],
                group(e),
            ).start()

    def back_inner(s, m):
        arrived(xr.at[4 + s, m, :, 0], x_r.at[4 + s, m])
        inner, inv = inner_all[s, rows(m), :], inv_all[s, rows(m), :]
        sig = jax.nn.sigmoid(inner)
        bi = x_total(4 + s, m, 0) * sig * (1.0 + inner * (1.0 - sig)) * inv
        bis = bi.astype(BF16)
        bis_all[s, rows(m), :] = bis
        coef = jnp.sum(bis.astype(F32) * inner * inv, axis=-1, keepdims=True) * (1.0 / WIDTH)
        return bis, jnp.broadcast_to(coef, (TOK, CH))

    def backward(s, m):
        bis, coef = back_inner(s, m)
        wide[...] = dot_t(bis, flat(s, DOWN))

        def step(kk, _):
            value = (
                ups[s, kk, rows(m), :].astype(F32)
                + wide[:, cols(kk)] * gain_row(s, kk)
                - acts[s, kk, rows(m), :].astype(F32) * coef
            )
            value = recode(value, GB[s - 1, kk, rows(m), :], LX[1, s - 1, kk, rows(m), :])
            ups[s - 1, kk, rows(m), :] = value
            narrow[:, cols(kk)] = value
            return 0

        chunk_loop(step, 0)
        xs[4 + s - 1, m, 0] = dot(narrow[...], flat(s - 1, UP)).astype(BF16)
        xb_send(s - 1, m)

    def make_grad_up(s):
        left = jnp.transpose(hid_all[s].astype(F32)).astype(BF16)

        def step(kk, _):
            G[s, UP, kk // 2, kk % 2] = dot(left, ups[s, kk]).astype(BF16)
            return 0

        chunk_loop(step, 0)

    def make_grad_down(s):
        left = jnp.transpose(bis_all[s].astype(F32)).astype(BF16)

        def step(kk, _):
            G[s, DOWN, kk // 2, kk % 2] = (dot(left, acts[s, kk]) * gain_row(s, kk)).astype(BF16)
            return 0

        chunk_loop(step, 0)

    def to_z(o):
        return ((z + o) % 4) // 2

    def z_give(view, there, kind, rs):
        def give(d):
            o = OFF[d]
            remote(view(to_z(o)), there.at[d], left.at[kind], rs, at_z(o)).start()

        @pl.when(src)
        def _():
            give(2)

        @pl.when(not_src)
        def _():
            give(0)
            give(1)

    rlow, rhigh = pl.ds(0, RANK // 2), pl.ds(RANK // 2, RANK // 2)

    def grad_down_last():
        make_grad_down(0)
        z_give(lambda i: G.at[0, DOWN, :, i, rlow], R1d.at[0, :, :, rlow], L_RA, r1_r.at[0, DOWN])
        for d, o in enumerate(OFF):
            remote(G.at[0, DOWN, (y + o) % 4, :, rhigh], R1h.at[d], left.at[L_RB], g1_r.at[0], at_y(o)).start()

    def send_grad_up(s):
        for d, o in SIDES:
            remote(G.at[s, UP, (y + 2) % 4, d], Qu.at[s, d], left.at[L_RU], q_r.at[s, UP], at_y(o)).start()
        for d, o in SIDES:
            remote(
                G.at[s, UP, (y + o) % 4, 1 - d], R1u.at[s, d, 1 - d], left.at[L_RU], r1_r.at[s, UP], at_y(o)
            ).start()

    def relay_up(s):
        arrived(Qu.at[s], q_r.at[s, UP])
        for d, o in SIDES:
            own = G[s, UP, (y + o) % 4, d].astype(F32)
            G[s, UP, (y + o) % 4, d] = (own + Qu[s, d].astype(F32)).astype(BF16)
            remote(
                G.at[s, UP, (y + o) % 4, d], R1u.at[s, d, d], left.at[L_RU], r1_r.at[s, UP], at_y(o)
            ).start()

    def send_grad_down(s):
        @pl.when(src)
        def _():
            for d, o in SIDES:
                remote(
                    G.at[s, DOWN, pair(d), 1 - i_own], Qd.at[s, d], left.at[L_RD], q_r.at[s, DOWN], at_z(o)
                ).start()

        @pl.when(not_src)
        def _():
            for d, o in SIDES:
                remote(
                    G.at[s, DOWN, pair(1 - d), to_z(o)],
                    R1d.at[s, d, pair(1 - d)],
                    left.at[L_RD],
                    r1_r.at[s, DOWN],
                    at_z(o),
                ).start()

    def relay_down(s):
        @pl.when(not_src)
        def _():
            arrived(Qd.at[s], q_r.at[s, DOWN])
            for d, o in SIDES:
                for k in range(2):
                    own = G[s, DOWN, 2 * d + k, to_z(o)].astype(F32)
                    G[s, DOWN, 2 * d + k, to_z(o)] = (own + Qd[s, d, k].astype(F32)).astype(BF16)
                remote(
                    G.at[s, DOWN, pair(d), to_z(o)],
                    R1d.at[s, d, pair(d)],
                    left.at[L_RD],
                    r1_r.at[s, DOWN],
                    at_z(o),
                ).start()

    def add_up(a, parts):
        total = a.astype(F32)
        for part in parts:
            total = total + part.astype(F32)
        return total.astype(BF16)

    def r2_up(s):
        arrived(R1u.at[s], r1_r.at[s, UP])
        for i in range(2):
            S1u[s, i] = add_up(G[s, UP, y, i], [R1u[s, d, i] for d in range(2)])
        z_give(lambda i: S1u.at[s, i], R2.at[s, UP], L_R2U, r2_r.at[s, UP])

    def r2_down(s):
        @pl.when(src)
        def _():
            arrived(R1d.at[s, 0:2], r1_r.at[s, DOWN])
            for yy in range(4):
                S1d[s, yy] = add_up(G[s, DOWN, yy, i_own], [R1d[s, d, yy] for d in range(2)])
            for d, o in enumerate(OFF):
                remote(
                    S1d.at[s, (y + o) % 4], R2.at[s, DOWN, d], left.at[L_R2D], r2_r.at[s, DOWN], at_y(o)
                ).start()

    def r2_last():
        @pl.when(src)
        def _():
            arrived(R1d.at[0, :, :, rlow], r1_r.at[0, DOWN])
            for yy in range(4):
                S1d[0, yy, rlow, :] = add_up(
                    G[0, DOWN, yy, i_own, rlow, :], [R1d[0, d, yy, rlow, :] for d in range(3)]
                )
            for d, o in enumerate(OFF):
                remote(
                    S1d.at[0, (y + o) % 4, rlow],
                    R2.at[0, DOWN, d, rlow],
                    left.at[L_R2L],
                    r2_r.at[0, DOWN],
                    at_y(o),
                ).start()

        arrived(R1h, g1_r.at[0])
        for i in range(2):
            S1h[i] = add_up(G[0, DOWN, y, i, rhigh, :], [R1h[d, i] for d in range(3)])
        z_give(lambda i: S1h.at[i], R2.at[0, DOWN, :, rhigh], L_R2L, r2_r.at[0, DOWN])

    def r3(s, mat):
        @pl.when(src)
        def _():
            arrived(R2.at[s, mat], r2_r.at[s, mat])
            if s == 0 and mat == DOWN:
                for part, own in ((rlow, S1d[s, y, rlow, :]), (rhigh, S1h[i_own])):
                    S2[s, mat, part, :] = add_up(own, [R2[s, mat, d, part, :] for d in range(3)])
            else:
                own = S1u[s, i_own] if mat == UP else S1d[s, y]
                S2[s, mat] = add_up(own, [R2[s, mat, d] for d in range(3)])

            @pl.when(jnp.logical_not(owner_self(s)))
            def _():
                remote(S2.at[s, mat], R3.at[xl, mat], left.at[L_R3], r3_r.at[mat], owner(s)).start()

            @pl.when(owner_self(s))
            def _():
                pltpu.make_async_copy(S2.at[s, mat], R3.at[xl, mat], r3_r.at[mat]).start()

    def base_ready(table, b, sems):
        arrived(table.at[b], sems.at[b])

    def drain():
        sent(gains.at[0:3], left.at[L_GAIN])
        sent(lims.at[0:3], left.at[L_LIM])
        pl.when(holds_mid)(lambda: sent(acts, left.at[L_BASE]))
        pl.when(lacks_mid)(lambda: sent(TB.at[0:2], left.at[L_BASE]))
        pl.when(src)(lambda: sent(W.at[0:3, 0], left.at[L_W1]))
        pl.when(src)(lambda: sent(R2.at[0:3, 0], left.at[L_W0]))
        pl.when(not_src)(lambda: sent(R2.at[0, 0], left.at[L_W0]))
        pl.when(src)(lambda: sent(W.at[0:3, 0], left.at[L_WD]))
        pl.when(not_src)(lambda: sent(W.at[0:3, 0, 0:2], left.at[L_WD]))
        sent(W.at[0:3, 0], left.at[L_WU])
        sent(W.at[0:3, 0], left.at[L_RU])
        pl.when(src)(lambda: sent(W.at[0:3, 0, 0:2], left.at[L_RD]))
        pl.when(not_src)(lambda: sent(W.at[0:3, 0], left.at[L_RD]))
        pl.when(src)(lambda: sent(W.at[0, 0, 0], left.at[L_RA]))
        pl.when(not_src)(lambda: sent(W.at[0, 0, 0:2], left.at[L_RA]))
        sent(R1h, left.at[L_RB])
        pl.when(src)(lambda: sent(W.at[0, 0, 0:2], left.at[L_R2U]))
        pl.when(not_src)(lambda: sent(W.at[0, 0], left.at[L_R2U]))
        pl.when(src)(lambda: sent(R2.at[0:3, 0], left.at[L_R2D]))
        pl.when(src)(lambda: sent(W.at[0, 0, 0], left.at[L_R2L]))
        pl.when(not_src)(lambda: sent(W.at[0, 0, 0, 0], left.at[L_R2L]))
        sent(xr.at[0:6], left.at[L_X])

    lax.fori_loop(0, CHUNKS, build_sel, 0)

    def p1_late():
        for mat in (DOWN, UP):
            for s in (2, 3):
                p1_send(s, mat)

    pl.when(xh == 1)(p1_late)
    p1_first()
    p1_send(1, DOWN)
    p1_send(0, UP)
    p1_send(1, UP)
    p0_left()
    t_bases()
    pl.when(xh == 0)(p1_late)
    p2_first()
    p2_down(1)
    p2_up(0)
    p2_down(2)
    p2_up(1)
    p2_up(2)
    g_bases()
    arrived(gains.at[0:3], gain_r.at[0])
    arrived(lims.at[0:3], lim_r.at[0])
    for s in range(3):
        spread(0, s)
    local_done(acts.at[0], loc_sem.at[0])
    first_ready()
    first(0)
    first(1)
    g_cross(0, 3)
    p3_down(1)
    p2_down(3)
    p3_down(2)
    base_ready(TB, 0, t_ready)
    order(TB, 0)
    up_ready(0)
    down_ready(1)
    forward(0, 0)
    p3_up(1)
    p2_up(3)
    forward(0, 1)
    g_cross(3, 6)
    p3_down(3)
    p3_up(2)
    base_ready(TB, 1, t_ready)
    order(TB, 1)
    up_ready(1)
    down_ready(2)
    forward(1, 0)
    p3_up(3)
    forward(1, 1)
    g_cross(6, CHUNKS)
    base_ready(TB, 2, t_ready)
    order(TB, 2)
    spread(1, 3)
    spread(1, 2)
    up_ready(2)
    down_ready(3)
    forward(2, 0)
    forward(2, 1)
    up_ready(3)
    local_done(ups.at[3], loc_sem.at[1])
    back_first(0)
    back_first(1)
    spread(1, 1)
    activate(3, 0)
    activate(3, 1)
    make_grad_up(3)
    send_grad_up(3)
    base_ready(GB, 2, g_ready)
    order(GB, 2)
    backward(3, 0)
    backward(3, 1)
    make_grad_down(3)
    send_grad_down(3)
    make_grad_up(2)
    send_grad_up(2)
    base_ready(GB, 1, g_ready)
    order(GB, 1)
    backward(2, 0)
    relay_up(3)
    backward(2, 1)
    make_grad_down(2)
    make_grad_up(1)
    relay_down(3)
    send_grad_down(2)
    relay_up(2)
    send_grad_up(1)
    base_ready(GB, 0, g_ready)
    order(GB, 0)
    backward(1, 0)
    r2_up(3)
    backward(1, 1)
    make_grad_down(1)
    make_grad_up(0)
    relay_down(2)
    send_grad_down(1)
    relay_up(1)
    send_grad_up(0)
    r2_down(3)
    r2_up(2)
    back_inner(0, 0)
    back_inner(0, 1)
    grad_down_last()
    relay_down(1)
    relay_up(0)
    r2_down(2)
    r2_up(1)
    r3(3, UP)
    r3(3, DOWN)
    r2_last()
    r2_up(0)
    r2_down(1)
    r3(2, UP)
    r3(2, DOWN)
    r3(1, UP)
    r3(0, DOWN)
    r3(0, UP)
    r3(1, DOWN)
    drain()

    scale = 1.0 / math.sqrt(2 * 2048)
    for mat in (UP, DOWN):
        arrived(R3.at[:, mat], r3_r.at[mat])
        total = (R3[0, mat].astype(F32) + R3[1, mat].astype(F32)) * scale
        out_ref[mat] = jnp.transpose(total)

    keeps_r3 = src & (xl == xh)
    pl.when(keeps_r3)(lambda: sent(W.at[0, 0, 0:3], left.at[L_R3]))
    pl.when(src & (xl != xh))(lambda: sent(W.at[0, 0], left.at[L_R3]))


def split(both_ref, down_ref, up_ref):
    down_ref[0] = both_ref[DOWN]
    up_ref[0] = both_ref[UP]


def body(
    inputs,
    cotangent,
    down_weight,
    up_weight,
    section_gains,
    act_bases,
    grad_bases,
    slot_ids,
    act_exps,
    grad_exps,
):
    any_spec = pl.BlockSpec(memory_space=pl.ANY)
    vmem = pl.BlockSpec(memory_space=pltpu.VMEM)
    dma = pltpu.SemaphoreType.DMA
    both = pl.pallas_call(
        kernel,
        out_shape=jax.ShapeDtypeStruct((2, CH, RANK), F32),
        in_specs=[any_spec] * 9 + [pl.BlockSpec(memory_space=pltpu.SMEM)],
        out_specs=vmem,
        scratch_shapes=[
            pltpu.VMEM((4, 2, 4, 2, CH, RANK), BF16),
            pltpu.VMEM((4, CHUNKS, ROWS, CH), BF16),
            pltpu.VMEM((4, CHUNKS, ROWS, CH), BF16),
            pltpu.VMEM((3, CHUNKS, ROWS, CH), BF16),
            pltpu.VMEM((3, CHUNKS, ROWS, CH), BF16),
            pltpu.VMEM((1, WIDTH), BF16),
            pltpu.VMEM((2, ROWS, 64), jnp.int32),
            pltpu.VMEM((4, 1, WIDTH), F32),
            pltpu.VMEM((4, ROWS, 128), BF16),
            pltpu.VMEM((2, CHUNKS, 128, CH), BF16),
            pltpu.VMEM((8, 2, 2, TOK, 128), BF16),
            pltpu.VMEM((8, 2, 3, 2, TOK, 128), BF16),
            pltpu.VMEM((4, ROWS, RANK), F32),
            pltpu.VMEM((4, ROWS, RANK), F32),
            pltpu.VMEM((4, ROWS, RANK), BF16),
            pltpu.VMEM((4, ROWS, RANK), BF16),
            pltpu.VMEM((4, 2, 4, 2, RANK, CH), BF16),
            pltpu.VMEM((4, 3, 4, RANK, CH), BF16),
            pltpu.VMEM((4, 2, 2, RANK, CH), BF16),
            pltpu.VMEM((4, 4, RANK, CH), BF16),
            pltpu.VMEM((4, 2, RANK, CH), BF16),
            pltpu.VMEM((4, 2, 3, RANK, CH), BF16),
            pltpu.VMEM((4, 2, RANK, CH), BF16),
            pltpu.VMEM((2, 2, RANK, CH), BF16),
            pltpu.VMEM((3, 2, RANK // 2, CH), BF16),
            pltpu.VMEM((2, RANK // 2, CH), BF16),
            pltpu.VMEM((4, 2, 2, RANK, CH), BF16),
            pltpu.VMEM((4, 2, RANK, CH), BF16),
            pltpu.VMEM((2, 3, CHUNKS, ROWS, CH), BF16),
            pltpu.VMEM((TOK, CHUNKS * CH), F32),
            pltpu.VMEM((TOK, CHUNKS * CH), BF16),
            dma((4,)),
            dma((3,)),
            dma((3,)),
            dma((1,)),
            dma((1,)),
            dma((4, 2)),
            dma((4, 2)),
            dma((1,)),
            dma((1,)),
            dma((4, 2)),
            dma((4,)),
            dma((4, 2)),
            dma((4, 2)),
            dma((1,)),
            dma((4, 2)),
            dma((2,)),
            dma((8, 2)),
            dma((LEFT_KINDS,)),
        ],
        compiler_params=pltpu.CompilerParams(
            collective_id=0, has_side_effects=True, vmem_limit_bytes=56 * 2**20
        ),
    )(
        inputs.reshape(ROWS, WIDTH),
        cotangent.reshape(ROWS, WIDTH),
        down_weight[0],
        up_weight[0],
        act_bases.reshape(2, ROWS, WIDTH),
        grad_bases.reshape(2, ROWS, WIDTH),
        section_gains,
        act_exps.reshape(ROWS, 64),
        grad_exps.reshape(ROWS, 64),
        slot_ids,
    )
    grad_down, grad_up = pl.pallas_call(
        split,
        out_shape=(jax.ShapeDtypeStruct((1, CH, RANK), F32),) * 2,
        in_specs=[vmem],
        out_specs=(vmem, vmem),
    )(both)
    return grad_down, grad_up


def solution(mesh):
    return jax.shard_map(
        body,
        mesh=mesh,
        in_specs=(
            P(None, "dp", None),
            P(None, "dp", None),
            P("section", "dp", None),
            P("section", "dp", None),
            P("section", None),
            P("section", None, None, "dp", None),
            P("section", None, None, "dp", None),
            P("dp", None),
            P("section", None, "dp", None),
            P("section", None, "dp", None),
        ),
        out_specs=(P("section", "dp", None), P("section", "dp", None)),
        check_vma=False,
    )
```

time: 99.5 us -> 89.6 us (0.901)
  Pallas kernels: 98.6 us -> 88.2 us
    pallas_call x1, Pallas kernels: 97 us -> 86.5 us  [body(): pl.pallas_call(kernel, out_shape=jax.ShapeDtypeStruct((2, CH, RANK), F32)...]
where the time goes in v3:
time: 89.6 us; the launch traced here: 88.8 us
  Pallas kernels  88.2 us (98%)
    pallas_call x1, Pallas kernels, body(): pl.pallas_call(kernel, out_shape=jax.ShapeDtypeStruct((2, CH, RANK), F32)...  86.5 us

profile of v3, /device:TPU:2, one launch (start us, length us, event | category | flops | bytes accessed | tf_op | source)
XLA Modules:
  0.0 88.8 jit_solution(16436292469411348895)
XLA Ops:
  0.6 86.5 %shard_map.113.both_ref = f32[2,256,128]{2,1,0:T(8,128)} custom-call(bf16[128,8192]{1,0:T(8,128)(2,1)} %bitcast.10, bf16[128,8192]{1,0:T(8,128)(2,1)} %bitcast.11, bf16[256,128]{1,0:T(8,128)(2,1)} %bitcast.12, bf16[256,128]{1,0:T(8,128)(2,1)} %bitcast.13, bf16[2,128,8192]{2,1,0:T(8,128)(2,1)} %bitcast.8, bf16[2,128,8192]{2,1,0:T(8,128)(2,1)} %bitcast.9, ...), custom_call_target="tpu_custom_call" | custom-call | tf_op jit(solution)/shard_map/pallas_call | solution.py:864
  87.2 1.7 %shard_map.114 = (f32[1,256,128]{2,1,0:T(8,128)}, f32[1,256,128]{2,1,0:T(8,128)}) custom-call(f32[2,256,128]{2,1,0:T(8,128)} %shard_map.113.both_ref), custom_call_target="tpu_custom_call" | custom-call | tf_op jit(solution)/shard_map/pallas_call | solution.py:935

commit v4 on v3

v4 whole, which is shorter than its diff:
```python
import functools
import math

import jax
import jax.numpy as jnp
from jax import lax
from jax.experimental import pallas as pl
from jax.experimental.pallas import tpu as pltpu
from jax.sharding import PartitionSpec as P

MESH = pl.DeviceIdType.MESH
F32 = jnp.float32
BF16 = jnp.bfloat16

SECTIONS = 4
WIDTH = 8192
RANK = 128
TOK = 64
ROWS = 2 * TOK
OWN = 256
BL = 128
BLOCKS = 16
CH = 2 * BL
CHUNKS = 8
NORM_EPS = 1e-05
OFF = (1, 3, 2)
DOWN, UP = 0, 1
(
    L_P0,
    L_GAIN,
    L_LIM,
    L_BASE,
    L_W1,
    L_W0,
    L_WD,
    L_WU,
    L_RU,
    L_RD,
    L_RA,
    L_R2,
    L_R3,
    L_X,
    L_XB,
    LEFT_KINDS,
) = range(16)


def dot(a, b):
    return jnp.dot(a, b, preferred_element_type=F32)


def dot_t(a, b):
    return lax.dot_general(a, b, (((1,), (1,)), ((), ())), preferred_element_type=F32)


def kernel(
    x_hbm,
    ct_hbm,
    dw_hbm,
    uw_hbm,
    ab_hbm,
    gb_hbm,
    gain_hbm,
    ae_hbm,
    ge_hbm,
    slot_ref,
    out_ref,
    W,
    acts,
    ups,
    TB,
    GB,
    gain_in,
    gain_out,
    exps_in,
    gains,
    lims,
    sel,
    xs,
    xr,
    inner_all,
    inv_all,
    hid_all,
    bis_all,
    G,
    Q,
    R1,
    S1,
    R1a,
    S1a,
    R1h,
    S1h,
    R2,
    S2,
    R3,
    LX,
    wide,
    narrow,
    loc_sem,
    t_ready,
    g_ready,
    gain_r,
    lim_r,
    p0_r,
    p1_r,
    h1_r,
    h2_r,
    p2_r,
    q_r,
    r1_r,
    a1_r,
    g1_r,
    r2_r,
    r3_r,
    x_r,
    left,
):
    S, J = lax.axis_index("section"), lax.axis_index("dp")
    xh, c = S // 2, S % 2
    y, xl, z = J // 8, (J // 4) % 2, J % 4

    def dp(yy, xx, zz):
        return yy * 8 + xx * 4 + zz

    def at_y(o):
        return (S, dp((y + o) % 4, xl, z))

    def at_z(o):
        return (S, dp(y, xl, (z + o) % 4))

    def group(e):
        return ((S + e) % 4, J)

    def p0_dev(xx, h):
        return (xl * 2 + h, dp(y, xx, z))

    def p0_self(xx, h):
        return (xl * 2 + h == S) & (xl == xx)

    def owner(s):
        return (s, dp(y, xh, z))

    def owner_self(s):
        return (S == s) & (xl == xh)

    def feat(k, h, cc):
        return (k // 4) * 2048 + h * 1024 + (k % 4) * OWN + cc * BL

    def remote(a, b, ss, rs, dev):
        return pltpu.make_async_remote_copy(
            src_ref=a, dst_ref=b, send_sem=ss, recv_sem=rs, device_id=dev, device_id_type=MESH
        )

    def arrived(ref, rs):
        remote(ref, ref, rs, rs, (S, J)).wait_recv()

    def sent(ref, ss):
        remote(ref, ref, ss, ss, (S, J)).wait_send()

    def local_done(ref, sem):
        pltpu.make_async_copy(ref, ref, sem).wait()

    barrier = pltpu.get_barrier_semaphore()

    def greet(dev):
        pl.semaphore_signal(barrier, inc=1, device_id=dev, device_id_type=MESH)

    def greet_all():
        for e in (1, 2, 3):
            greet(group(e))
            greet(at_y(e))
            greet(at_z(e))
        for xx in (0, 1):
            for h in (0, 1):
                @pl.when(jnp.logical_not(p0_self(xx, h)))
                def _():
                    greet(p0_dev(xx, h))
        for s in range(SECTIONS):
            @pl.when(jnp.logical_not(owner_self(s)))
            def _():
                greet(owner(s))

    def place(ref_of, dst, k, h, cc):
        return (
            ref_of.at[:, pl.ds(pl.multiple_of(feat(k, h, cc), BL), BL)],
            dst.at[k // 2, :, pl.ds(pl.multiple_of((k % 2) * BL, BL), BL)],
        )

    def load(ref_of, dst, sem, h, cc):
        def step(k, _):
            pltpu.make_async_copy(*place(ref_of, dst, k, h, cc), sem).start()
            return 0

        lax.fori_loop(0, BLOCKS, step, 0)

    def push(ref_of, dst, ss, rs, h, cc, dev, lo, hi):
        def step(k, _):
            remote(*place(ref_of, dst, k, h, cc), ss, rs, dev).start()
            return 0

        lax.fori_loop(lo, hi, step, 0)

    near = 2 * xh
    holds_mid = c != xh
    lacks_mid = c == xh
    cross = (S + 2) % 4
    sib = xh * 2 + (1 - c)

    greet_all()
    pltpu.make_async_copy(gain_hbm, gain_in, loc_sem.at[2]).start()
    pltpu.make_async_copy(ae_hbm, exps_in.at[0], loc_sem.at[3]).start()
    pltpu.make_async_copy(ge_hbm, exps_in.at[1], loc_sem.at[3]).start()
    load(x_hbm, acts.at[0], loc_sem.at[0], xh, c)
    pl.semaphore_wait(barrier, 9 + 8 - 2 * jnp.where(xl == xh, 1, 0))

    def p0_send():
        for mat, ref in ((DOWN, dw_hbm), (UP, uw_hbm)):
            for xx in (0, 1):
                for h in (0, 1):
                    here, there = ref.at[pl.ds(h * BL, BL)], W.at[S, mat, y, z]

                    @pl.when(jnp.logical_not(p0_self(xx, h)))
                    def _():
                        remote(here, there, left.at[L_P0], p0_r.at[S, mat], p0_dev(xx, h)).start()

                    @pl.when(p0_self(xx, h))
                    def _():
                        pltpu.make_async_copy(here, there, p0_r.at[S, mat]).start()

    pl.when(c == 0)(p0_send)

    pltpu.make_async_copy(gain_hbm, gain_in, loc_sem.at[2]).wait()
    for dst in range(SECTIONS):
        for kk in range(CHUNKS):
            for j in (0, 1):
                row = gain_in[:, pl.ds(feat(2 * kk + j, dst // 2, dst % 2), BL)].astype(F32)
                gain_out[dst, pl.ds(kk, 1), pl.ds(j * BL, BL)] = row
    gains[S] = gain_out[S]
    local_done(exps_in, loc_sem.at[3])
    exps = jnp.concatenate([exps_in[0], exps_in[1]], axis=1)
    limit = jnp.full((ROWS, 128), 448.0 * 2.0**-6, F32)
    for e in (7, 8, 9):
        limit = jnp.where(exps == e, 448.0 * 2.0**-e, limit)
    lims[S] = limit.astype(BF16)
    pl.when(c == 1)(p0_send)
    for e in (1, 2, 3):
        remote(gain_out.at[(S + e) % 4], gains.at[S], left.at[L_GAIN], gain_r.at[0], group(e)).start()
        remote(lims.at[S], lims.at[S], left.at[L_LIM], lim_r.at[0], group(e)).start()

    def build_sel(kk, _):
        b0 = (kk // 2) * 16 + xh * 8 + (kk % 2) * 4 + c
        row = lax.broadcasted_iota(jnp.int32, (128, CH), 0)
        blk = (lax.broadcasted_iota(jnp.int32, (128, CH), 1) // BL) * 2 + b0
        sel[0, kk] = jnp.where(row == blk, 1.0, 0.0).astype(BF16)
        sel[1, kk] = jnp.where(row == blk + 64, 1.0, 0.0).astype(BF16)
        return 0

    def t_bases():
        push(ab_hbm.at[1 - c], TB.at[near], left.at[L_BASE], t_ready.at[near], 1 - xh, c, (cross, J), 0, BLOCKS)
        load(ab_hbm.at[1 - c], TB.at[near], t_ready.at[near], xh, c)

        @pl.when(holds_mid)
        def _():
            push(ab_hbm.at[c], TB.at[1], left.at[L_BASE], t_ready.at[1], xh, 1 - c, (sib, J), 0, BLOCKS)
            load(ab_hbm.at[c], TB.at[1], t_ready.at[1], xh, c)

    def g_bases():
        load(ct_hbm, ups.at[3], loc_sem.at[1], xh, c)
        load(gb_hbm.at[1 - c], GB.at[near], g_ready.at[near], xh, c)

        @pl.when(holds_mid)
        def _():
            push(gb_hbm.at[c], GB.at[1], left.at[L_BASE], g_ready.at[1], xh, 1 - c, (sib, J), 0, BLOCKS)
            load(gb_hbm.at[c], GB.at[1], g_ready.at[1], xh, c)

    def g_cross(lo, hi):
        push(gb_hbm.at[1 - c], GB.at[near], left.at[L_BASE], g_ready.at[near], 1 - xh, c, (cross, J), lo, hi)

    def p0_left():
        pl.when(xl == xh)(lambda: sent(W.at[0, 0, 0:2, 0:3], left.at[L_P0]))
        pl.when(xl != xh)(lambda: sent(W.at[0, 0, 0:2], left.at[L_P0]))

    half = BL // 2
    low, high = pl.ds(0, half), pl.ds(half, half)
    SIDES = ((0, 1), (1, 3))

    def p1_send(s, mat):
        w = W.at[s, mat, y, z]
        arrived(w, p0_r.at[s, mat])
        for o in OFF:
            there = at_y(o) if mat == DOWN else at_z(o)
            remote(w, w, left.at[L_W1], p1_r.at[s, mat], there).start()

    def p1_first(s, mat, i):
        w = W.at[s, mat, y, z]
        arrived(w, p0_r.at[s, mat])
        for o in OFF:
            v = w.at[low]
            remote(v, v, left.at[L_W1], p1_r.at[s, mat], at_y(o)).start()
            v = w.at[high]
            remote(v, v, left.at[L_W1], h1_r.at[i], at_z(o)).start()

    def p2_first(s, mat, i):
        arrived(W.at[s, mat, 0:3, 0, low], p1_r.at[s, mat])
        for o in OFF:
            w = W.at[s, mat, :, z, low]
            remote(w, w, left.at[L_W0], p2_r.at[s, mat], at_z(o)).start()
        arrived(W.at[s, mat, 0, 0:3, high], h1_r.at[i])
        for o in OFF:
            w = W.at[s, mat, y, :, high]
            remote(w, w, left.at[L_W0], h2_r.at[i], at_y(o)).start()

    def first_ready(s, mat, i):
        arrived(W.at[s, mat, :, 0:3, low], p2_r.at[s, mat])
        arrived(W.at[s, mat, 0:3, :, high], h2_r.at[i])

    def p2_down(s):
        arrived(W.at[s, DOWN, 0:3, 0], p1_r.at[s, DOWN])
        for o in OFF:
            w = W.at[s, DOWN, :, z]
            remote(w, w, left.at[L_WD], p2_r.at[s, DOWN], at_z(o)).start()

    def down_ready(s):
        arrived(W.at[s, DOWN, :, 0:3], p2_r.at[s, DOWN])

    def p2_up(s):
        arrived(W.at[s, UP, 0, 0:3], p1_r.at[s, UP])
        for o in OFF:
            w = W.at[s, UP, y]
            remote(w, w, left.at[L_WU], p2_r.at[s, UP], at_y(o)).start()

    def up_ready(s):
        arrived(W.at[s, UP, 0:3], p2_r.at[s, UP])

    def pair(d):
        return pl.ds(2 * d, 2)

    def rows(m):
        return pl.ds(m * TOK, TOK)

    def gain_row(s, kk):
        return gains[s, pl.ds(kk, 1), :]

    def rows_of(s, mat, kk):
        return W[s, mat, kk // 2, pl.ds((kk % 2) * 2, 2)].reshape(CH, RANK)

    def fold(v):
        return v[:, :128] + v[:, 128:]

    def chunk_loop(step, init):
        return lax.fori_loop(0, CHUNKS, step, init, unroll=True)

    def x_send(ex, m):
        for e in (1, 2, 3):
            remote(
                xs.at[ex, m], xr.at[ex, m, e - 1], left.at[L_X], x_r.at[ex, m], group(e)
            ).start()

    inner_rows, square_rows = pl.ds(0, TOK), pl.ds(TOK, 16)

    def x_total(ex, m, part):
        total = xs[ex, m, part, :].astype(F32)
        for e in range(3):
            total = total + xr[ex, m, e, part, :].astype(F32)
        return total

    def diagonal(v):
        shape = (TOK, 128)
        here = lax.broadcasted_iota(jnp.int32, shape, 0) == lax.broadcasted_iota(jnp.int32, shape, 1)
        return jnp.where(here, v, 0.0)

    def x_wait(ex, m):
        arrived(xr.at[ex, m], x_r.at[ex, m])

    zero = jnp.zeros((TOK, 128), F32)

    def enter(s, kk, value, inner, sq):
        full = value.astype(F32)
        sq = sq + fold(full * full)
        scaled = (full * gain_row(s, kk)).astype(BF16)
        return inner + dot(scaled, rows_of(s, DOWN, kk)), sq

    def hand_over(ex, m, inner, sq):
        row = jnp.sum(diagonal(jnp.sum(sq, axis=-1, keepdims=True)), axis=0, keepdims=True)
        coarse = row.astype(BF16).astype(F32)
        upper = lax.broadcasted_iota(jnp.int32, (16, 128), 0) < 8
        xs[ex, m, inner_rows, :] = inner.astype(BF16)
        xs[ex, m, square_rows, :] = jnp.where(upper, coarse, row - coarse).astype(BF16)
        x_send(ex, m)

    def first(m):
        def step(kk, carry):
            return enter(0, kk, acts[0, kk, rows(m), :], *carry)

        inner, sq = chunk_loop(step, (zero, zero))
        hand_over(0, m, inner, sq)

    def activate(s, m):
        x_wait(s, m)
        squares = x_total(s, m, square_rows)
        row = squares[0:1, :] + squares[8:9, :]
        mean = jnp.sum(diagonal(row), axis=-1, keepdims=True) * (1.0 / WIDTH)
        inv = jnp.broadcast_to(lax.rsqrt(mean + NORM_EPS), (TOK, 128))
        inner = x_total(s, m, inner_rows) * inv
        hid = (inner * jax.nn.sigmoid(inner)).astype(BF16)
        inner_all[s, rows(m), :] = inner
        inv_all[s, rows(m), :] = inv
        hid_all[s, rows(m), :] = hid
        return hid

    def spread(t, s):
        def step(kk, _):
            LX[t, s - t, kk] = dot(lims[s], sel[t, kk]).astype(BF16)
            return 0

        chunk_loop(step, 0)

    def order(table, b):
        straight = jnp.full((TOK, CH), slot_ref[0, 0]) == 0

        def step(kk, _):
            one = table[b, kk, 0:TOK, :].astype(F32)
            two = table[b, kk, TOK:ROWS, :].astype(F32)
            table[b, kk, 0:TOK, :] = jnp.where(straight, one, two).astype(BF16)
            table[b, kk, TOK:ROWS, :] = jnp.where(straight, two, one).astype(BF16)
            return 0

        chunk_loop(step, 0)

    def recode(value, base, limit):
        base, limit = base.astype(F32), limit.astype(F32)
        delta = jnp.minimum(jnp.maximum(value - base, -limit), limit).astype(BF16)
        return (base + delta.astype(F32)).astype(BF16)

    def cols(kk):
        return pl.ds(pl.multiple_of(kk * CH, CH), CH)

    def flat(s, mat):
        return W[s, mat].reshape(CHUNKS * CH, RANK)

    def forward(s, m):
        hid = activate(s, m)
        wide[...] = dot_t(hid, flat(s, UP))

        def step(kk, sq):
            out = acts[s, kk, rows(m), :].astype(F32) + wide[:, cols(kk)]
            value = recode(out, TB[s, kk, rows(m), :], LX[0, s, kk, rows(m), :])
            acts[s + 1, kk, rows(m), :] = value
            full = value.astype(F32)
            narrow[:, cols(kk)] = (full * gain_row(s + 1, kk)).astype(BF16)
            return sq + fold(full * full)

        sq = chunk_loop(step, zero)
        hand_over(s + 1, m, dot(narrow[...], flat(s + 1, DOWN)), sq)

    def back_first(m):
        def step(kk, carry):
            return carry + dot(ups[3, kk, rows(m), :], rows_of(3, UP, kk))

        xs[4 + 3, m, inner_rows, :] = chunk_loop(step, zero).astype(BF16)
        xb_send(3, m)

    def xb_send(s, m):
        for e in (1, 2, 3):
            remote(
                xs.at[4 + s, m, inner_rows],
                xr.at[4 + s, m, e - 1, inner_rows],
                left.at[L_XB],
                x_r.at[4 + s, m],
                group(e),
            ).start()

    def back_inner(s, m):
        arrived(xr.at[4 + s, m, :, inner_rows], x_r.at[4 + s, m])
        inner, inv = inner_all[s, rows(m), :], inv_all[s, rows(m), :]
        sig = jax.nn.sigmoid(inner)
        bi = x_total(4 + s, m, inner_rows) * sig * (1.0 + inner * (1.0 - sig)) * inv
        bis = bi.astype(BF16)
        bis_all[s, rows(m), :] = bis
        coef = jnp.sum(bis.astype(F32) * inner * inv, axis=-1, keepdims=True) * (1.0 / WIDTH)
        return bis, jnp.broadcast_to(coef, (TOK, CH))

    def backward(s, m):
        bis, coef = back_inner(s, m)
        wide[...] = dot_t(bis, flat(s, DOWN))

        def step(kk, _):
            value = (
                ups[s, kk, rows(m), :].astype(F32)
                + wide[:, cols(kk)] * gain_row(s, kk)
                - acts[s, kk, rows(m), :].astype(F32) * coef
            )
            value = recode(value, GB[s - 1, kk, rows(m), :], LX[1, s - 1, kk, rows(m), :])
            ups[s - 1, kk, rows(m), :] = value
            narrow[:, cols(kk)] = value
            return 0

        chunk_loop(step, 0)
        xs[4 + s - 1, m, inner_rows, :] = dot(narrow[...], flat(s - 1, UP)).astype(BF16)
        xb_send(s - 1, m)

    def keep(s, mat, kk, value):
        value = value.astype(BF16)
        G[s, mat, kk // 2, (kk % 2) * 2] = value[:, :BL]
        G[s, mat, kk // 2, (kk % 2) * 2 + 1] = value[:, BL:]

    def make_grad_up(s):
        turned = jnp.transpose(hid_all[s].astype(F32)).astype(BF16)

        def step(kk, _):
            keep(s, UP, kk, dot(turned, ups[s, kk]))
            return 0

        chunk_loop(step, 0)

    def make_grad_down(s):
        turned = jnp.transpose(bis_all[s].astype(F32)).astype(BF16)

        def step(kk, _):
            keep(s, DOWN, kk, dot(turned, acts[s, kk]) * gain_row(s, kk))
            return 0

        chunk_loop(step, 0)

    rlow, rhigh = pl.ds(0, RANK // 2), pl.ds(RANK // 2, RANK // 2)

    def part(s, mat, o, which):
        if mat == UP:
            return G.at[s, UP, (y + o) % 4, which]
        return G.at[s, DOWN, which, (z + o) % 4]

    def ring(mat):
        return at_y if mat == UP else at_z

    def kind(mat):
        return left.at[L_RU] if mat == UP else left.at[L_RD]

    def grad_down_last():
        make_grad_down(0)
        for d, o in enumerate(OFF):
            remote(
                G.at[0, DOWN, :, (z + o) % 4, rlow], R1a.at[d], left.at[L_RA], a1_r.at[0], at_z(o)
            ).start()
            remote(
                G.at[0, DOWN, (y + o) % 4, :, rhigh], R1h.at[d], left.at[L_RA], g1_r.at[0], at_y(o)
            ).start()

    def send_grad(s, mat):
        for d, o in SIDES:
            remote(part(s, mat, 2, pair(d)), Q.at[s, mat, d], kind(mat), q_r.at[s, mat], ring(mat)(o)).start()
        for d, o in SIDES:
            remote(
                part(s, mat, o, pair(1 - d)),
                R1.at[s, mat, d, pair(1 - d)],
                kind(mat),
                r1_r.at[s, mat],
                ring(mat)(o),
            ).start()

    def relay(s, mat):
        arrived(Q.at[s, mat], q_r.at[s, mat])
        for d, o in SIDES:
            for j in range(2):
                ref = part(s, mat, o, 2 * d + j)
                ref[...] = (ref[...].astype(F32) + Q[s, mat, d, j].astype(F32)).astype(BF16)
            remote(
                part(s, mat, o, pair(d)), R1.at[s, mat, d, pair(d)], kind(mat), r1_r.at[s, mat], ring(mat)(o)
            ).start()

    def add_up(a, parts):
        total = a.astype(F32)
        for value in parts:
            total = total + value.astype(F32)
        return total.astype(BF16)

    def r2(s, mat):
        arrived(R1.at[s, mat], r1_r.at[s, mat])
        for j in range(4):
            S1[s, mat, j] = add_up(part(s, mat, 0, j)[...], [R1[s, mat, d, j] for d in range(2)])
        for d, o in enumerate(OFF):
            there, j = (at_z(o), (z + o) % 4) if mat == UP else (at_y(o), (y + o) % 4)
            remote(S1.at[s, mat, j], R2.at[s, mat, d], left.at[L_R2], r2_r.at[s, mat], there).start()

    def r2_last():
        arrived(R1a, a1_r.at[0])
        for j in range(4):
            S1a[j] = add_up(G[0, DOWN, j, z, rlow, :], [R1a[d, j] for d in range(3)])
        for d, o in enumerate(OFF):
            remote(
                S1a.at[(y + o) % 4], R2.at[0, DOWN, d, rlow], left.at[L_R2], r2_r.at[0, DOWN], at_y(o)
            ).start()
        arrived(R1h, g1_r.at[0])
        for j in range(4):
            S1h[j] = add_up(G[0, DOWN, y, j, rhigh, :], [R1h[d, j] for d in range(3)])
        for d, o in enumerate(OFF):
            remote(
                S1h.at[(z + o) % 4], R2.at[0, DOWN, d, rhigh], left.at[L_R2], r2_r.at[0, DOWN], at_z(o)
            ).start()

    def r3(s, mat):
        arrived(R2.at[s, mat], r2_r.at[s, mat])
        if s == 0 and mat == DOWN:
            for some, own in ((rlow, S1a[y]), (rhigh, S1h[z])):
                S2[s, mat, some, :] = add_up(own, [R2[s, mat, d, some, :] for d in range(3)])
        else:
            own = S1[s, mat, z if mat == UP else y]
            S2[s, mat] = add_up(own, [R2[s, mat, d] for d in range(3)])

        @pl.when(jnp.logical_not(owner_self(s)))
        def _():
            remote(S2.at[s, mat], R3.at[xl, c, mat], left.at[L_R3], r3_r.at[mat], owner(s)).start()

        @pl.when(owner_self(s))
        def _():
            pltpu.make_async_copy(S2.at[s, mat], R3.at[xl, c, mat], r3_r.at[mat]).start()

    def base_ready(table, b, sems):
        arrived(table.at[b], sems.at[b])

    def drain():
        p0_left()
        sent(gains.at[0:3], left.at[L_GAIN])
        sent(lims.at[0:3], left.at[L_LIM])
        pl.when(holds_mid)(lambda: sent(acts, left.at[L_BASE]))
        pl.when(lacks_mid)(lambda: sent(TB.at[0:2], left.at[L_BASE]))
        sent(W.at[0:3, 0, 0:2], left.at[L_W1])
        sent(W.at[0:3, 0, 0:2], left.at[L_W0])
        sent(W.at[0:3, 0, 0:3], left.at[L_WD])
        sent(W.at[0:3, 0, 0:3], left.at[L_WU])
        sent(W.at[0:3, 0], left.at[L_RU])
        sent(W.at[0:3, 0, 0:3], left.at[L_RD])
        sent(W.at[0, 0, 0:3], left.at[L_RA])
        sent(W.at[0:3, 0, 0:2], left.at[L_R2])
        sent(xr.at[0:4], left.at[L_X])
        sent(xr.at[4:8, :, :, inner_rows], left.at[L_XB])

    lax.fori_loop(0, CHUNKS, build_sel, 0)

    def p1_late():
        p1_send(2, DOWN)
        p1_send(3, DOWN)
        p1_send(2, UP)
        p1_first(3, UP, 1)

    t_bases()
    holds_late = (xh == 1) & (xl == 1)
    pl.when(holds_late)(p1_late)
    p1_first(0, DOWN, 0)
    p1_send(1, DOWN)
    p1_send(0, UP)
    p1_send(1, UP)
    pl.when(jnp.logical_not(holds_late))(p1_late)
    p2_first(0, DOWN, 0)
    p2_up(0)
    p2_down(1)
    g_bases()
    arrived(gains.at[0:3], gain_r.at[0])
    arrived(lims.at[0:3], lim_r.at[0])
    for s in range(3):
        spread(0, s)
    p2_up(1)
    local_done(acts.at[0], loc_sem.at[0])
    first_ready(0, DOWN, 0)
    first(0)
    first(1)
    p2_down(2)
    p2_up(2)
    p2_down(3)
    p2_first(3, UP, 1)
    g_cross(0, 6)
    for s in range(3):
        base_ready(TB, s, t_ready)
        order(TB, s)
        if s == 2:
            spread(1, 3)
            spread(1, 2)
        up_ready(s)
        down_ready(s + 1)
        forward(s, 0)
        forward(s, 1)
        if s < 2:
            g_cross(6 * s + 6, min(6 * s + 12, BLOCKS))
    first_ready(3, UP, 1)
    local_done(ups.at[3], loc_sem.at[1])
    back_first(0)
    back_first(1)
    spread(1, 1)
    activate(3, 0)
    activate(3, 1)
    make_grad_up(3)
    send_grad(3, UP)
    base_ready(GB, 2, g_ready)
    order(GB, 2)
    backward(3, 0)
    backward(3, 1)
    make_grad_down(3)
    send_grad(3, DOWN)
    make_grad_up(2)
    send_grad(2, UP)
    base_ready(GB, 1, g_ready)
    order(GB, 1)
    relay(3, UP)
    backward(2, 0)
    backward(2, 1)
    make_grad_down(2)
    make_grad_up(1)
    relay(3, DOWN)
    send_grad(2, DOWN)
    relay(2, UP)
    send_grad(1, UP)
    base_ready(GB, 0, g_ready)
    order(GB, 0)
    r2(3, UP)
    backward(1, 0)
    backward(1, 1)
    make_grad_down(1)
    make_grad_up(0)
    r2(3, DOWN)
    relay(2, DOWN)
    send_grad(1, DOWN)
    send_grad(0, UP)
    relay(1, UP)
    back_inner(0, 0)
    back_inner(0, 1)
    grad_down_last()
    r2(2, UP)
    relay(0, UP)
    relay(1, DOWN)
    r2(2, DOWN)
    r2(1, UP)
    r2_last()
    r2(0, UP)
    r2(1, DOWN)
    r3(3, UP)
    r3(3, DOWN)
    r3(2, UP)
    r3(2, DOWN)
    r3(1, UP)
    r3(0, DOWN)
    r3(0, UP)
    r3(1, DOWN)
    drain()

    scale = 1.0 / math.sqrt(2 * 2048)
    for mat in (UP, DOWN):
        arrived(R3.at[:, :, mat], r3_r.at[mat])
        for h in (0, 1):
            total = (R3[0, h, mat].astype(F32) + R3[1, h, mat].astype(F32)) * scale
            out_ref[mat, pl.ds(h * BL, BL), :] = jnp.transpose(total)

    pl.when(xl == xh)(lambda: sent(W.at[0, 0, 0:2, 0:3], left.at[L_R3]))
    pl.when(xl != xh)(lambda: sent(W.at[0, 0, 0:2], left.at[L_R3]))


def split(both_ref, down_ref, up_ref):
    down_ref[0] = both_ref[DOWN]
    up_ref[0] = both_ref[UP]


def body(
    inputs,
    cotangent,
    down_weight,
    up_weight,
    section_gains,
    act_bases,
    grad_bases,
    slot_ids,
    act_exps,
    grad_exps,
):
    any_spec = pl.BlockSpec(memory_space=pl.ANY)
    vmem = pl.BlockSpec(memory_space=pltpu.VMEM)
    dma = pltpu.SemaphoreType.DMA
    both = pl.pallas_call(
        kernel,
        out_shape=jax.ShapeDtypeStruct((2, OWN, RANK), F32),
        in_specs=[any_spec] * 9 + [pl.BlockSpec(memory_space=pltpu.SMEM)],
        out_specs=vmem,
        scratch_shapes=[
            pltpu.VMEM((4, 2, 4, 4, BL, RANK), BF16),
            pltpu.VMEM((4, CHUNKS, ROWS, CH), BF16),
            pltpu.VMEM((4, CHUNKS, ROWS, CH), BF16),
            pltpu.VMEM((3, CHUNKS, ROWS, CH), BF16),
            pltpu.VMEM((3, CHUNKS, ROWS, CH), BF16),
            pltpu.VMEM((1, WIDTH), BF16),
            pltpu.VMEM((4, CHUNKS, CH), F32),
            pltpu.VMEM((2, ROWS, 64), jnp.int32),
            pltpu.VMEM((4, CHUNKS, CH), F32),
            pltpu.VMEM((4, ROWS, 128), BF16),
            pltpu.VMEM((2, CHUNKS, 128, CH), BF16),
            pltpu.VMEM((8, 2, TOK + 16, 128), BF16),
            pltpu.VMEM((8, 2, 3, TOK + 16, 128), BF16),
            pltpu.VMEM((4, ROWS, RANK), F32),
            pltpu.VMEM((4, ROWS, RANK), F32),
            pltpu.VMEM((4, ROWS, RANK), BF16),
            pltpu.VMEM((4, ROWS, RANK), BF16),
            pltpu.VMEM((4, 2, 4, 4, RANK, BL), BF16),
            pltpu.VMEM((4, 2, 2, 2, RANK, BL), BF16),
            pltpu.VMEM((4, 2, 2, 4, RANK, BL), BF16),
            pltpu.VMEM((4, 2, 4, RANK, BL), BF16),
            pltpu.VMEM((3, 4, RANK // 2, BL), BF16),
            pltpu.VMEM((4, RANK // 2, BL), BF16),
            pltpu.VMEM((3, 4, RANK // 2, BL), BF16),
            pltpu.VMEM((4, RANK // 2, BL), BF16),
            pltpu.VMEM((4, 2, 3, RANK, BL), BF16),
            pltpu.VMEM((4, 2, RANK, BL), BF16),
            pltpu.VMEM((2, 2, 2, RANK, BL), BF16),
            pltpu.VMEM((2, 3, CHUNKS, ROWS, CH), BF16),
            pltpu.VMEM((TOK, CHUNKS * CH), F32),
            pltpu.VMEM((TOK, CHUNKS * CH), BF16),
            dma((4,)),
            dma((3,)),
            dma((3,)),
            dma((1,)),
            dma((1,)),
            dma((4, 2)),
            dma((4, 2)),
            dma((2,)),
            dma((2,)),
            dma((4, 2)),
            dma((4, 2)),
            dma((4, 2)),
            dma((1,)),
            dma((1,)),
            dma((4, 2)),
            dma((2,)),
            dma((8, 2)),
            dma((LEFT_KINDS,)),
        ],
        compiler_params=pltpu.CompilerParams(
            collective_id=0, has_side_effects=True, vmem_limit_bytes=56 * 2**20
        ),
    )(
        inputs.reshape(ROWS, WIDTH),
        cotangent.reshape(ROWS, WIDTH),
        down_weight[0],
        up_weight[0],
        act_bases.reshape(2, ROWS, WIDTH),
        grad_bases.reshape(2, ROWS, WIDTH),
        section_gains,
        act_exps.reshape(ROWS, 64),
        grad_exps.reshape(ROWS, 64),
        slot_ids,
    )
    grad_down, grad_up = pl.pallas_call(
        split,
        out_shape=(jax.ShapeDtypeStruct((1, OWN, RANK), F32),) * 2,
        in_specs=[vmem],
        out_specs=(vmem, vmem),
    )(both)
    return grad_down, grad_up


def solution(mesh):
    return jax.shard_map(
        body,
        mesh=mesh,
        in_specs=(
            P(None, "dp", None),
            P(None, "dp", None),
            P("section", "dp", None),
            P("section", "dp", None),
            P("section", None),
            P("section", None, None, "dp", None),
            P("section", None, None, "dp", None),
            P("dp", None),
            P("section", None, "dp", None),
            P("section", None, "dp", None),
        ),
        out_specs=(P("section", "dp", None), P("section", "dp", None)),
        check_vma=False,
    )
```

time: 89.6 us -> 84.7 us (0.945)
  the two profiles are of different devices: /device:TPU:2 before, /device:TPU:1 now
where the time goes in v4:
time: 84.7 us; the launch traced here: 84.6 us
  Pallas kernels  83.9 us (99%)
    pallas_call x1, Pallas kernels, body(): pl.pallas_call(kernel, out_shape=jax.ShapeDtypeStruct((2, OWN, RANK), F32...  82.3 us

profile of v4, /device:TPU:1, one launch (start us, length us, event | category | flops | bytes accessed | tf_op | source)
XLA Modules:
  0.0 84.6 jit_solution(198691783889224309)
XLA Ops:
  0.6 82.3 %shard_map.113.both_ref = f32[2,256,128]{2,1,0:T(8,128)} custom-call(bf16[128,8192]{1,0:T(8,128)(2,1)} %bitcast.10, bf16[128,8192]{1,0:T(8,128)(2,1)} %bitcast.11, bf16[256,128]{1,0:T(8,128)(2,1)} %bitcast.12, bf16[256,128]{1,0:T(8,128)(2,1)} %bitcast.13, bf16[2,128,8192]{2,1,0:T(8,128)(2,1)} %bitcast.8, bf16[2,128,8192]{2,1,0:T(8,128)(2,1)} %bitcast.9, ...), custom_call_target="tpu_custom_call" | custom-call | tf_op jit(solution)/shard_map/pallas_call | solution.py:775
  82.9 1.7 %shard_map.114 = (f32[1,256,128]{2,1,0:T(8,128)}, f32[1,256,128]{2,1,0:T(8,128)}) custom-call(f32[2,256,128]{2,1,0:T(8,128)} %shard_map.113.both_ref), custom_call_target="tpu_custom_call" | custom-call | tf_op jit(solution)/shard_map/pallas_call | solution.py:846

commit v5 on v4

--- a/solution.py
+++ b/solution.py
@@ -64,7 +64,7 @@
     ae_hbm,
     ge_hbm,
     slot_ref,
-    out_ref,
+    out_hbm,
     W,
     acts,
     ups,
@@ -96,6 +96,8 @@
     LX,
     wide,
     narrow,
+    result,
+    out_sem,
     loc_sem,
     t_ready,
     g_ready,
@@ -213,21 +215,21 @@
     load(x_hbm, acts.at[0], loc_sem.at[0], xh, c)
     pl.semaphore_wait(barrier, 9 + 8 - 2 * jnp.where(xl == xh, 1, 0))
 
-    def p0_send():
-        for mat, ref in ((DOWN, dw_hbm), (UP, uw_hbm)):
-            for xx in (0, 1):
-                for h in (0, 1):
-                    here, there = ref.at[pl.ds(h * BL, BL)], W.at[S, mat, y, z]
-
-                    @pl.when(jnp.logical_not(p0_self(xx, h)))
-                    def _():
-                        remote(here, there, left.at[L_P0], p0_r.at[S, mat], p0_dev(xx, h)).start()
-
-                    @pl.when(p0_self(xx, h))
-                    def _():
-                        pltpu.make_async_copy(here, there, p0_r.at[S, mat]).start()
-
-    pl.when(c == 0)(p0_send)
+    def p0_send(mat):
+        ref = dw_hbm if mat == DOWN else uw_hbm
+        for xx in (0, 1):
+            for h in (0, 1):
+                here, there = ref.at[pl.ds(h * BL, BL)], W.at[S, mat, y, z]
+
+                @pl.when(jnp.logical_not(p0_self(xx, h)))
+                def _():
+                    remote(here, there, left.at[L_P0], p0_r.at[S, mat], p0_dev(xx, h)).start()
+
+                @pl.when(p0_self(xx, h))
+                def _():
+                    pltpu.make_async_copy(here, there, p0_r.at[S, mat]).start()
+
+    pl.when(c == 0)(lambda: p0_send(DOWN))
 
     pltpu.make_async_copy(gain_hbm, gain_in, loc_sem.at[2]).wait()
     for dst in range(SECTIONS):
@@ -242,7 +244,8 @@
     for e in (7, 8, 9):
         limit = jnp.where(exps == e, 448.0 * 2.0**-e, limit)
     lims[S] = limit.astype(BF16)
-    pl.when(c == 1)(p0_send)
+    pl.when(c == 1)(lambda: p0_send(DOWN))
+    p0_send(UP)
     for e in (1, 2, 3):
         remote(gain_out.at[(S + e) % 4], gains.at[S], left.at[L_GAIN], gain_r.at[0], group(e)).start()
         remote(lims.at[S], lims.at[S], left.at[L_LIM], lim_r.at[0], group(e)).start()
@@ -636,23 +639,27 @@
 
     lax.fori_loop(0, CHUNKS, build_sel, 0)
 
-    def p1_late():
+    def p1_second():
         p1_send(2, DOWN)
+        p1_send(2, UP)
+
+    def p1_third():
         p1_send(3, DOWN)
-        p1_send(2, UP)
         p1_first(3, UP, 1)
 
     t_bases()
     holds_late = (xh == 1) & (xl == 1)
-    pl.when(holds_late)(p1_late)
+    pl.when(holds_late)(p1_second)
+    pl.when(holds_late)(p1_third)
     p1_first(0, DOWN, 0)
     p1_send(1, DOWN)
     p1_send(0, UP)
     p1_send(1, UP)
-    pl.when(jnp.logical_not(holds_late))(p1_late)
+    pl.when(jnp.logical_not(holds_late))(p1_second)
     p2_first(0, DOWN, 0)
     p2_up(0)
     p2_down(1)
+    pl.when(jnp.logical_not(holds_late))(p1_third)
     g_bases()
     arrived(gains.at[0:3], gain_r.at[0])
     arrived(lims.at[0:3], lim_r.at[0])
@@ -665,8 +672,6 @@
     first(1)
     p2_down(2)
     p2_up(2)
-    p2_down(3)
-    p2_first(3, UP, 1)
     g_cross(0, 6)
     for s in range(3):
         base_ready(TB, s, t_ready)
@@ -678,6 +683,9 @@
         down_ready(s + 1)
         forward(s, 0)
         forward(s, 1)
+        if s == 0:
+            p2_down(3)
+            p2_first(3, UP, 1)
         if s < 2:
             g_cross(6 * s + 6, min(6 * s + 12, BLOCKS))
     first_ready(3, UP, 1)
@@ -710,9 +718,9 @@
     send_grad(1, UP)
     base_ready(GB, 0, g_ready)
     order(GB, 0)
-    r2(3, UP)
     backward(1, 0)
     backward(1, 1)
+    r2(3, UP)
     make_grad_down(1)
     make_grad_up(0)
     r2(3, DOWN)
@@ -723,22 +731,22 @@
     back_inner(0, 0)
     back_inner(0, 1)
     grad_down_last()
-    r2(2, UP)
     relay(0, UP)
     relay(1, DOWN)
+    r2(2, UP)
     r2(2, DOWN)
     r2(1, UP)
     r2_last()
+    r2(1, DOWN)
     r2(0, UP)
-    r2(1, DOWN)
     r3(3, UP)
     r3(3, DOWN)
     r3(2, UP)
     r3(2, DOWN)
     r3(1, UP)
     r3(0, DOWN)
+    r3(1, DOWN)
     r3(0, UP)
-    r3(1, DOWN)
     drain()
 
     scale = 1.0 / math.sqrt(2 * 2048)
@@ -746,10 +754,13 @@
         arrived(R3.at[:, :, mat], r3_r.at[mat])
         for h in (0, 1):
             total = (R3[0, h, mat].astype(F32) + R3[1, h, mat].astype(F32)) * scale
-            out_ref[mat, pl.ds(h * BL, BL), :] = jnp.transpose(total)
+            result[mat, pl.ds(h * BL, BL), :] = jnp.transpose(total)
+        pltpu.make_async_copy(result.at[mat], out_hbm.at[mat], out_sem.at[mat]).start()
 
     pl.when(xl == xh)(lambda: sent(W.at[0, 0, 0:2, 0:3], left.at[L_R3]))
     pl.when(xl != xh)(lambda: sent(W.at[0, 0, 0:2], left.at[L_R3]))
+    for mat in (UP, DOWN):
+        pltpu.make_async_copy(result.at[mat], out_hbm.at[mat], out_sem.at[mat]).wait()
 
 
 def split(both_ref, down_ref, up_ref):
@@ -776,7 +787,7 @@
         kernel,
         out_shape=jax.ShapeDtypeStruct((2, OWN, RANK), F32),
         in_specs=[any_spec] * 9 + [pl.BlockSpec(memory_space=pltpu.SMEM)],
-        out_specs=vmem,
+        out_specs=any_spec,
         scratch_shapes=[
             pltpu.VMEM((4, 2, 4, 4, BL, RANK), BF16),
             pltpu.VMEM((4, CHUNKS, ROWS, CH), BF16),
@@ -809,6 +820,8 @@
             pltpu.VMEM((2, 3, CHUNKS, ROWS, CH), BF16),
             pltpu.VMEM((TOK, CHUNKS * CH), F32),
             pltpu.VMEM((TOK, CHUNKS * CH), BF16),
+            pltpu.VMEM((2, OWN, RANK), F32),
+            dma((2,)),
             dma((4,)),
             dma((3,)),
             dma((3,)),

time: 84.7 us -> 82.9 us (0.979)
  the two profiles are of different devices: /device:TPU:1 before, /device:TPU:2 now
where the time goes in v5:
time: 82.9 us; the launch traced here: 82.7 us
  Pallas kernels  82 us (99%)
    pallas_call x1, Pallas kernels, body(): pl.pallas_call(kernel, out_shape=jax.ShapeDtypeStruct((2, OWN, RANK), F32...  80.4 us
    pallas_call x1, Pallas kernels, body(): pl.pallas_call(split, out_shape=(jax.ShapeDtypeStruct((1, OWN, RANK), F32...  1.66 us

profile of v5, /device:TPU:2, one launch (start us, length us, event | category | flops | bytes accessed | tf_op | source)
XLA Modules:
  0.0 82.7 jit_solution(11690959329980029595)
XLA Ops:
  0.6 80.4 %shard_map.113.both_ref = f32[2,256,128]{2,1,0:T(8,128)} custom-call(bf16[128,8192]{1,0:T(8,128)(2,1)} %bitcast.10, bf16[128,8192]{1,0:T(8,128)(2,1)} %bitcast.11, bf16[256,128]{1,0:T(8,128)(2,1)} %bitcast.12, bf16[256,128]{1,0:T(8,128)(2,1)} %bitcast.13, bf16[2,128,8192]{2,1,0:T(8,128)(2,1)} %bitcast.8, bf16[2,128,8192]{2,1,0:T(8,128)(2,1)} %bitcast.9, ...), custom_call_target="tpu_custom_call" | custom-call | tf_op jit(solution)/shard_map/pallas_call | solution.py:786
  81.0 1.7 %shard_map.114 = (f32[1,256,128]{2,1,0:T(8,128)}, f32[1,256,128]{2,1,0:T(8,128)}) custom-call(f32[2,256,128]{2,1,0:T(8,128)} %shard_map.113.both_ref), custom_call_target="tpu_custom_call" | custom-call | tf_op jit(solution)/shard_map/pallas_call | solution.py:859

commit v6 on v5

--- a/solution.py
+++ b/solution.py
@@ -97,6 +97,8 @@
     wide,
     narrow,
     result,
+    held,
+    held_sem,
     out_sem,
     loc_sem,
     t_ready,
@@ -208,6 +210,8 @@
     cross = (S + 2) % 4
     sib = xh * 2 + (1 - c)
 
+    for mat, ref in ((DOWN, dw_hbm), (UP, uw_hbm)):
+        pltpu.make_async_copy(ref, held.at[mat], held_sem.at[mat]).start()
     greet_all()
     pltpu.make_async_copy(gain_hbm, gain_in, loc_sem.at[2]).start()
     pltpu.make_async_copy(ae_hbm, exps_in.at[0], loc_sem.at[3]).start()
@@ -216,10 +220,9 @@
     pl.semaphore_wait(barrier, 9 + 8 - 2 * jnp.where(xl == xh, 1, 0))
 
     def p0_send(mat):
-        ref = dw_hbm if mat == DOWN else uw_hbm
         for xx in (0, 1):
             for h in (0, 1):
-                here, there = ref.at[pl.ds(h * BL, BL)], W.at[S, mat, y, z]
+                here, there = held.at[mat, pl.ds(h * BL, BL)], W.at[S, mat, y, z]
 
                 @pl.when(jnp.logical_not(p0_self(xx, h)))
                 def _():
@@ -229,6 +232,7 @@
                 def _():
                     pltpu.make_async_copy(here, there, p0_r.at[S, mat]).start()
 
+    local_done(held.at[DOWN], held_sem.at[DOWN])
     pl.when(c == 0)(lambda: p0_send(DOWN))
 
     pltpu.make_async_copy(gain_hbm, gain_in, loc_sem.at[2]).wait()
@@ -245,6 +249,7 @@
         limit = jnp.where(exps == e, 448.0 * 2.0**-e, limit)
     lims[S] = limit.astype(BF16)
     pl.when(c == 1)(lambda: p0_send(DOWN))
+    local_done(held.at[UP], held_sem.at[UP])
     p0_send(UP)
     for e in (1, 2, 3):
         remote(gain_out.at[(S + e) % 4], gains.at[S], left.at[L_GAIN], gain_r.at[0], group(e)).start()
@@ -354,7 +359,7 @@
         return lax.fori_loop(0, CHUNKS, step, init, unroll=True)
 
     def x_send(ex, m):
-        for e in (1, 2, 3):
+        for e in (2, 3, 1):
             remote(
                 xs.at[ex, m], xr.at[ex, m, e - 1], left.at[L_X], x_r.at[ex, m], group(e)
             ).start()
@@ -464,7 +469,7 @@
         xb_send(3, m)
 
     def xb_send(s, m):
-        for e in (1, 2, 3):
+        for e in (2, 3, 1):
             remote(
                 xs.at[4 + s, m, inner_rows],
                 xr.at[4 + s, m, e - 1, inner_rows],
@@ -724,23 +729,23 @@
     make_grad_down(1)
     make_grad_up(0)
     r2(3, DOWN)
-    relay(2, DOWN)
     send_grad(1, DOWN)
     send_grad(0, UP)
-    relay(1, UP)
     back_inner(0, 0)
     back_inner(0, 1)
     grad_down_last()
+    relay(2, DOWN)
+    relay(1, UP)
+    r3(3, UP)
+    r3(3, DOWN)
     relay(0, UP)
     relay(1, DOWN)
     r2(2, UP)
+    r2_last()
     r2(2, DOWN)
     r2(1, UP)
-    r2_last()
     r2(1, DOWN)
     r2(0, UP)
-    r3(3, UP)
-    r3(3, DOWN)
     r3(2, UP)
     r3(2, DOWN)
     r3(1, UP)
@@ -821,6 +826,8 @@
             pltpu.VMEM((TOK, CHUNKS * CH), F32),
             pltpu.VMEM((TOK, CHUNKS * CH), BF16),
             pltpu.VMEM((2, OWN, RANK), F32),
+            pltpu.VMEM((2, OWN, RANK), BF16),
+            dma((2,)),
             dma((2,)),
             dma((4,)),
             dma((3,)),

time: 82.9 us -> 83 us (level)
  no operation moved by 1% of the time
where the time goes in v6:
time: 83 us; the launch traced here: 82.8 us
  Pallas kernels  82.2 us (99%)
    pallas_call x1, Pallas kernels, body(): pl.pallas_call(kernel, out_shape=jax.ShapeDtypeStruct((2, OWN, RANK), F32...  80.5 us

profile of v6, /device:TPU:2, one launch (start us, length us, event | category | flops | bytes accessed | tf_op | source)
XLA Modules:
  0.0 82.8 jit_solution(2239256384460032016)
XLA Ops:
  0.6 80.5 %shard_map.113.both_ref = f32[2,256,128]{2,1,0:T(8,128)} custom-call(bf16[128,8192]{1,0:T(8,128)(2,1)} %bitcast.10, bf16[128,8192]{1,0:T(8,128)(2,1)} %bitcast.11, bf16[256,128]{1,0:T(8,128)(2,1)} %bitcast.12, bf16[256,128]{1,0:T(8,128)(2,1)} %bitcast.13, bf16[2,128,8192]{2,1,0:T(8,128)(2,1)} %bitcast.8, bf16[2,128,8192]{2,1,0:T(8,128)(2,1)} %bitcast.9, ...), custom_call_target="tpu_custom_call" | custom-call | tf_op jit(solution)/shard_map/pallas_call | solution.py:791
  81.1 1.7 %shard_map.114 = (f32[1,256,128]{2,1,0:T(8,128)}, f32[1,256,128]{2,1,0:T(8,128)}) custom-call(f32[2,256,128]{2,1,0:T(8,128)} %shard_map.113.both_ref), custom_call_target="tpu_custom_call" | custom-call | tf_op jit(solution)/shard_map/pallas_call | solution.py:866
